TPU v7x, 256 devices: a whole 4x4x8 slice. The times are simulated.
256 devices in a mesh: dp: 16 (over z_hi, x), seq: 16 (over z_lo, y, core).
Axes of the slice: x: 4, y: 4, z: 8 (z_hi: 4, z_lo: 2; z = z_hi * 2 + z_lo), core: 2. Of those that a mesh axis runs over, the one named last changes fastest.
Arguments:
- patches: bfloat16 [16, 4096, 1280], P('dp', 'seq'), may hold values from -72 to 72
- image_ids: int32 [16, 4096], P('dp'), may hold values from 0 to 3, never falling along the last dimension, each value on 1 to 2048 neighbouring positions
- w_qkv: bfloat16 [3, 1280, 1280], P(None, 'dp', 'seq'), may hold values from -0.15625 to 0.15625
- w_out: bfloat16 [1280, 1280], P('seq', 'dp'), may hold values from -0.3125 to 0.3125
Outputs:
- attended: bfloat16 [16, 4096, 1280], P('dp', 'seq')
Inputs may be any that keep to these rules, and one draw needn't show every extreme that they name: `image_ids`: image numbers never fall along a row; each image has 1 to 2048 patches, one of them exactly that many.
All inputs are finite; a program needn't handle non-finite values.
Results may differ from a plain program's by a relative error of at most 0.0055.
The roundings to bfloat16 on the way count: a program that leaves them out, or rounds other values in their place, can miss the bound.
Values may be sent and summed in bfloat16 or wider, within the bound.
A program may use at most 64 MiB of HBM per device.

v0:
```python
import jax
import jax.numpy as jnp
from jax import lax
from jax.sharding import PartitionSpec as P

HD = 80


def attend(query, keys, values, ids):
    total = query.shape[0]
    width = query.shape[1]
    nheads = width // HD
    block = min(512, total)
    qh = query.reshape(total, nheads, HD)
    kh = keys.reshape(total, nheads, HD)
    vh = values.reshape(total, nheads, HD)

    def one_block(index):
        start = index * block
        qblock = lax.dynamic_slice_in_dim(qh, start, block, 0)
        idblock = lax.dynamic_slice_in_dim(ids, start, block, 0)
        scores = jnp.einsum(
            "qhd,khd->hqk", qblock, kh, preferred_element_type=jnp.float32
        ) / jnp.sqrt(jnp.float32(HD))
        same = idblock[:, None] == ids[None, :]
        scores = jnp.where(same[None], scores, jnp.float32(-1e30))
        top = jnp.max(scores, axis=-1, keepdims=True)
        expd = jnp.exp(scores - top)
        probs = (expd / jnp.sum(expd, axis=-1, keepdims=True)).astype(jnp.bfloat16)
        outs = jnp.einsum("hqk,khd->qhd", probs, vh, preferred_element_type=jnp.float32)
        return outs.astype(jnp.bfloat16).reshape(block, width)

    blocks = lax.map(one_block, jnp.arange(total // block, dtype=jnp.int32))
    return blocks.reshape(total, width)


def shards(patches, image_ids, w_qkv, w_out):
    proj_cols, out_rows = (
        lax.all_gather(w_qkv, "dp", axis=1, tiled=True),
        lax.all_gather(w_out, "dp", axis=1, tiled=True),
    )
    ids = image_ids[0]
    local_rows = patches.shape[1]
    proj = jnp.einsum(
        "sd,tdc->tsc",
        lax.all_gather(patches, "seq", axis=1, tiled=True)[0],
        proj_cols,
        preferred_element_type=jnp.float32,
    ).astype(jnp.bfloat16)
    heads_out = attend(proj[0], proj[1], proj[2], ids)
    summed = lax.psum_scatter(
        jnp.dot(heads_out, out_rows, preferred_element_type=jnp.float32),
        "seq",
        scatter_dimension=0,
        tiled=True,
    )
    return summed.astype(jnp.bfloat16).reshape(1, local_rows, summed.shape[1])


def solution(mesh):
    return jax.shard_map(
        shards,
        mesh=mesh,
        in_specs=(P("dp", "seq", None), P("dp", None), P(None, "dp", "seq"), P("seq", "dp")),
        out_specs=P("dp", "seq", None),
        check_vma=False,
    )
```

profile of v0, /device:TPU:1, one launch (start us, length us, event | category | flops | bytes accessed | tf_op | source)
XLA Modules:
  0.0 311.2 jit_solution(12434050727713099878)
XLA Ops:
  9.0 43.5 %all_gather.11 = bf16[80,1280]{0,1:T(8,128)(2,1)S(1)} all-gather(bf16[80,80]{0,1:T(8,128)(2,1)S(1)} %copy.14), channel_id=1, replica_groups=mesh['dp'=16,'seq'=16] {'dp'}, dimensions={1}, use_global_device_ids=true | all-gather | bytes 217600 | tf_op jit(solution)/shard_map/all_gather | solution.py:40
  52.6 54.6 %all_gather.9 = bf16[3,1280,80]{2,0,1:T(4,128)(2,1)S(1)} all-gather(bf16[3,80,80]{2,0,1:T(4,128)(2,1)S(1)} %copy.11), channel_id=1, replica_groups=mesh['dp'=16,'seq'=16] {'dp'}, dimensions={1}, use_global_device_ids=true | all-gather | bytes 652800 | tf_op jit(solution)/shard_map/all_gather | solution.py:39
  107.1 8.3 %fusion.15 = bf16[3,4096,80]{1,2,0:T(8,128)(2,1)S(1)} fusion(bf16[1,4096,1280]{2,1,0:T(8,128)(2,1)} %all-gather.2.cloned.1.call-done, bf16[3,1280,80]{2,0,1:T(4,128)(2,1)S(1)} %all_gather.9), kind=kOutput, calls=%fused_computation.16 | convolution fusion | flops 2517565440 | bytes 13066240 | tf_op jit(solution)/shard_map/sd,tdc->tsc/dot_general | solution.py:44
  115.7 51.5 %while.10 = (s32[]{:T(128)}, bf16[8,512,80]{1,2,0:T(8,128)(2,1)S(1)}, s32[8]{0:T(128)S(1)}, s32[4096]{0:T(1024)S(1)}, s32[1,4096]{1,0:T(1,128)S(1)}, /*index=5*/...) while((s32[]{:T(128)}, ...), condition=%wide.region_3.4_spmd, body=%wide.region_0.3_spmd.sunk | while | flops 690002944 | bytes 26673348 | solution.py:33
  117.0 1.7 fusion.28
  118.8 1.3 fusion.29
  120.1 2.1 fusion.30
  123.5 1.7 fusion.28
  126.5 2.1 fusion.30
  129.9 1.7 fusion.28
  132.9 2.1 fusion.30
  136.3 1.7 fusion.28
  139.3 2.1 fusion.30
  142.8 1.7 fusion.28
  145.8 2.1 fusion.30
  149.2 1.7 fusion.28
  152.2 2.1 fusion.30
  155.6 1.7 fusion.28
  158.6 2.1 fusion.30
  162.1 1.7 fusion.28
  165.1 2.1 fusion.30
  167.2 8.6 %fusion.20 = f32[4096,1280]{1,0:T(8,128)} fusion(bf16[4096,80]{0,1:T(8,128)(2,1)S(1)} %bitcast.60, bf16[80,1280]{0,1:T(8,128)(2,1)S(1)} %all_gather.11), kind=kOutput, calls=%fused_computation.23 | convolution fusion | flops 838860800 | bytes 21831680 | tf_op jit(solution)/shard_map/dot_general | solution.py:52
  175.8 126.4 %reduce-scatter.2.cloned.1.call-done = f32[256,1280]{1,0:T(8,128)} async-done(((f32[4096,1280]{1,0:T(8,128)}), f32[256,1280]{1,0:T(8,128)}) %reduce-scatter.2.cloned.1.call-update) | async-done | bytes 1310736 | tf_op jit(solution)/shard_map/reduce_scatter | solution.py:51
  302.2 2.2 convert_bitcast_fusion
  (36 shorter events, 17.2 us)
Async XLA Ops:
  6.5 100.6 %all-gather.2.cloned.1.call-start = ((), (), s32[]{:S(2)}) async-start(), calls=%async_computation.1 | async-start | bytes 11141120 | tf_op jit(solution)/shard_map/all_gather | solution.py:46
  7.3 294.9 %reduce-scatter.2.cloned.1.call-start = ((), (), s32[]{:S(2)}) async-start(), calls=%async_computation.2 | async-start | bytes 22282240 | tf_op jit(solution)/shard_map/reduce_scatter | solution.py:51
  107.1 8.6 %copy-start = (s32[1,4096]{1,0:T(1,128)S(1)}, s32[1,4096]{1,0:T(1,128)}, u32[]{:S(2)}) copy-start(s32[1,4096]{1,0:T(1,128)} %param.7) | copy-start | bytes 49156
Sparse Core Ops, SparseCore 0:
  9.2 95.5 all-gather.1
  175.9 126.2 reduce-scatter.1
where the time goes:
time: 312 us; the launch traced here: 311 us
  waiting for transfers between devices  127 us (41%)
  blocking collectives  98.1 us (31%)
  matrix products  47.2 us (15%)
  between operations  13.5 us (4%)
  other arithmetic  12.5 us (4%)
  local copies, waits for them, and re-layouts  7.47 us (2%)
  loops' own time  5.35 us (2%)
    reduce_scatter x1, waiting for transfers between devices, shards(): lax.psum_scatter(jnp.dot(heads_out, out_rows, preferred_element_type=jnp....  126 us
    all_gather x1, blocking collectives, shards(): lax.all_gather(w_qkv, 'dp', axis=1, tiled=True)  54.6 us
    all_gather x1, blocking collectives, shards(): lax.all_gather(w_out, 'dp', axis=1, tiled=True)  43.5 us
    dot_general x8, matrix products, one_block(): jnp.einsum('hqk,khd->qhd', probs, vh, preferred_element_type=jnp.float32)  16.5 us
    dot_general x8, matrix products, one_block(): jnp.einsum('qhd,khd->hqk', qblock, kh, preferred_element_type=jnp.float32)  13.8 us
    reduce_sum x8, other arithmetic, one_block(): probs = (expd / jnp.sum(expd, axis=-1, keepdims=True)).astype(jnp.bfloat16)  10.3 us
    dot_general x1, matrix products, shards(): jnp.dot(heads_out, out_rows, preferred_element_type=jnp.float32)  8.56 us
    dot_general x1, matrix products, shards(): jnp.einsum('sd,tdc->tsc', lax.all_gather(patches, 'seq', axis=1, tiled=Tr...  8.34 us
  transfers between devices with their start and end apart: 2, of which 1 were waited for; matrix products, arithmetic and copies ran while one was open for 1% of the time, Pallas kernels for 0%

commit v1 on v0

v1 whole, which is shorter than its diff:
```python
import functools
import math

import jax
import jax.numpy as jnp
from jax import lax
from jax.experimental import pallas as pl
from jax.experimental.pallas import tpu as pltpu
from jax.sharding import PartitionSpec as P

MESH = pl.DeviceIdType.MESH
HD = 80
D = 1280
ROWS = 256
SEQ = 4096
PACK = 256
BF16 = jnp.bfloat16
F32 = jnp.float32


def place():
    dp, sq = lax.axis_index("dp"), lax.axis_index("seq")
    x = lax.rem(dp, 4)
    y = lax.rem(lax.div(sq, 2), 4)
    z = lax.div(dp, 4) * 2 + lax.div(sq, 8)
    return x, y, z, lax.rem(sq, 2)


def device(x, y, z, c):
    return (lax.div(z, 2) * 4 + x, lax.rem(z, 2) * 8 + y * 2 + c)


def project_kernel(x_ref, w_ref, qkv_ref, xbuf, wbuf, pbuf, ssem, rsem, lsem):
    x, y, z, c = place()
    zl = lax.rem(z, 2)
    xp, xm, x2 = lax.rem(x + 1, 4), lax.rem(x + 3, 4), lax.rem(x + 2, 4)
    yp, ym, y2 = lax.rem(y + 1, 4), lax.rem(y + 3, 4), lax.rem(y + 2, 4)
    zp, zm = lax.rem(z + 1, 8), lax.rem(z + 7, 8)
    co = 1 - c
    mate = z + 1 - 2 * zl
    to_xp, to_xm = device(xp, y, z, c), device(xm, y, z, c)
    to_yp, to_ym = device(x, yp, z, c), device(x, ym, z, c)
    to_zp, to_zm = device(x, y, zp, c), device(x, y, zm, c)
    to_co, to_mate = device(x, y, z, co), device(x, y, mate, c)

    barrier = pltpu.get_barrier_semaphore()
    for to in (to_xp, to_xm, to_yp, to_ym, to_zp, to_zm, to_co):
        pl.semaphore_signal(barrier, inc=1, device_id=to, device_id_type=MESH)
    pl.semaphore_wait(barrier, 7)

    sent = []

    def copy(src, dst, k, to):
        return pltpu.make_async_remote_copy(
            src_ref=src,
            dst_ref=dst,
            send_sem=ssem.at[k],
            recv_sem=rsem.at[k],
            device_id=to,
            device_id_type=MESH,
        )

    def send(src, dst, k, to):
        cp = copy(src, dst, k, to)
        cp.start()
        sent.append(cp)

    def arrived(dst, k):
        copy(dst, dst, k, to_co).wait_recv()

    def wslot(zz, xx):
        row = pl.multiple_of((lax.div(zz, 2) * 4 + xx) * HD, 16)
        return wbuf.at[lax.rem(zz, 2), pl.ds(row, HD), :]

    def zslot(j):
        return lax.rem(z + 8 - j, 8) if j <= 4 else lax.rem(z + j - 4, 8)

    def xid(j, k):
        return 7 + 3 * j + k

    half = ROWS // 2

    def xpart(cc, yy, part):
        return xbuf.at[cc, yy, pl.ds(part * half, half), :]

    send(w_ref, wslot(z, x), 0, to_zp)
    send(w_ref, wslot(z, x), 4, to_zm)
    send(w_ref, wslot(z, x), xid(0, 0), to_xp)
    send(w_ref, wslot(z, x), xid(0, 1), to_xm)
    for part in (0, 1):
        src = x_ref.at[pl.ds(part * half, half), :]
        send(src, xpart(c, y, part), 31 + part, to_yp)
        src = x_ref.at[pl.ds((1 - part) * half, half), :]
        send(src, xpart(c, y, 1 - part), 34 - part, to_ym)
    send(x_ref, xbuf.at[c, y], 37, to_co)
    own_w = pltpu.make_async_copy(w_ref, wslot(z, x), lsem.at[8])
    own_w.start()
    own_x = pltpu.make_async_copy(x_ref, xbuf.at[c, y], lsem.at[9])
    own_x.start()

    def x_forward(j):
        zz = zslot(j)
        if j % 2 == 0:
            arrived(wslot(zz, xm), xid(j, 0))
            send(wslot(zz, xm), wslot(zz, xm), xid(j, 2), to_xp)
        else:
            arrived(wslot(zz, xp), xid(j, 1))
            send(wslot(zz, xp), wslot(zz, xp), xid(j, 2), to_xm)

    before = 0
    for j in (1, 5, 2, 6, 3, 7, 4):
        here = wslot(zslot(j), x)
        arrived(here, j - 1)
        if j in (1, 2, 3):
            send(here, here, j, to_zp)
        if j in (5, 6):
            send(here, here, j, to_zm)
        send(here, here, xid(j, 0), to_xp)
        send(here, here, xid(j, 1), to_xm)
        x_forward(before)
        before = j
    x_forward(before)

    arrived(xpart(c, ym, 0), 31)
    send(xpart(c, ym, 0), xpart(c, ym, 0), 35, to_yp)
    arrived(xpart(c, yp, 1), 34)
    send(xpart(c, yp, 1), xpart(c, yp, 1), 36, to_ym)

    for j in range(8):
        zz = zslot(j)
        if j % 2 == 0:
            arrived(wslot(zz, xp), xid(j, 1))
        else:
            arrived(wslot(zz, xm), xid(j, 0))
        arrived(wslot(zz, x2), xid(j, 2))
    own_w.wait()

    kept = []

    def block(cc, yy):
        source = zl * 8 + yy * 2 + cc
        return qkv_ref.at[pl.ds(pl.multiple_of(source * ROWS, ROWS), ROWS), :]

    def project(i, cc, yy):
        patches = xbuf[cc, yy]
        for whose, head in ((0, 1 - zl), (1, zl)):
            pbuf[i, whose] = jnp.dot(
                patches, wbuf[head], preferred_element_type=F32
            ).astype(BF16)
            if whose == 0:
                send(pbuf.at[i, 0], block(cc, yy), 41 + i, to_mate)
            else:
                keep = pltpu.make_async_copy(pbuf.at[i, 1], block(cc, yy), lsem.at[i])
                keep.start()
                kept.append(keep)

    own_x.wait()
    project(0, c, y)
    arrived(xbuf.at[co, y], 37)
    project(1, co, y)
    arrived(xpart(c, ym, 1), 32)
    send(xbuf.at[c, ym], xbuf.at[c, ym], 38, to_co)
    arrived(xpart(c, yp, 0), 33)
    send(xbuf.at[c, yp], xbuf.at[c, yp], 39, to_co)
    project(2, c, ym)
    project(3, c, yp)
    arrived(xbuf.at[co, ym], 38)
    project(4, co, ym)
    arrived(xbuf.at[co, yp], 39)
    project(5, co, yp)
    arrived(xpart(c, y2, 0), 35)
    arrived(xpart(c, y2, 1), 36)
    send(xbuf.at[c, y2], xbuf.at[c, y2], 40, to_co)
    project(6, c, y2)
    arrived(xbuf.at[co, y2], 40)
    project(7, co, y2)

    theirs = 1 - zl
    for i, (cc, yy) in enumerate(
        ((c, y), (co, y), (c, ym), (c, yp), (co, ym), (co, yp), (c, y2), (co, y2))
    ):
        source = theirs * 8 + yy * 2 + cc
        dst = qkv_ref.at[pl.ds(pl.multiple_of(source * ROWS, ROWS), ROWS), :]
        arrived(dst, 41 + i)
    for keep in kept:
        keep.wait()
    for cp in sent:
        cp.wait_send()


def project(patches, w):
    return pl.pallas_call(
        project_kernel,
        out_shape=jax.ShapeDtypeStruct((SEQ, PACK), BF16),
        in_specs=[
            pl.BlockSpec(memory_space=pl.ANY),
            pl.BlockSpec(memory_space=pltpu.VMEM),
        ],
        out_specs=pl.BlockSpec(memory_space=pl.ANY),
        scratch_shapes=[
            pltpu.VMEM((2, 4, ROWS, D), BF16),
            pltpu.VMEM((2, D, PACK), BF16),
            pltpu.VMEM((8, 2, ROWS, PACK), BF16),
            pltpu.SemaphoreType.DMA((49,)),
            pltpu.SemaphoreType.DMA((49,)),
            pltpu.SemaphoreType.DMA((10,)),
        ],
        compiler_params=pltpu.CompilerParams(
            collective_id=0, has_side_effects=True, vmem_limit_bytes=40 << 20
        ),
        name="project",
    )(patches, w)


TQ = 256
CK = 512
SCALE = math.log2(math.e) / math.sqrt(HD)


def fold(op, a):
    parts = [a[:, i : i + 128] for i in range(0, a.shape[1], 128)]
    while len(parts) > 1:
        parts = [op(parts[i], parts[i + 1]) for i in range(0, len(parts), 2)]
    return parts[0]


def attend_kernel(ids_ref, qkv_ref, o_ref, kaug, scores):
    ids = ids_ref[...]
    cuts = [
        jnp.sum((ids < a).astype(F32)).astype(jnp.int32) for a in (1, 2, 3)
    ]

    def image_of(start, rows):
        pos = lax.broadcasted_iota(jnp.int32, (rows, 128), 0) + start
        return sum((pos >= cut).astype(jnp.int32) for cut in cuts)

    lane = lax.broadcasted_iota(jnp.int32, (TQ, 128), 1)

    @pl.loop(0, SEQ // TQ)
    def _(i):
        rows = pl.ds(pl.multiple_of(i * TQ, TQ), TQ)
        keys = qkv_ref[rows, 128:256].astype(F32)
        other = jnp.where(image_of(i * TQ, TQ) != lane - HD, 1.0, 0.0)
        kaug[rows, :] = jnp.where(lane < HD, keys, other).astype(BF16)

    @pl.loop(0, SEQ // TQ)
    def _(i):
        first = i * TQ
        rows = pl.ds(pl.multiple_of(first, TQ), TQ)
        lo, hi = jnp.int32(0), jnp.int32(SEQ)
        for cut in cuts:
            lo = jnp.maximum(lo, jnp.where(cut <= first, cut, 0))
            hi = jnp.minimum(hi, jnp.where(cut >= first + TQ, cut, SEQ))
        j0, j1 = lax.div(lo, CK), lax.div(hi + CK - 1, CK)
        query = qkv_ref[rows, 0:128].astype(F32)
        own = jnp.where(image_of(first, TQ) == lane - HD, -1e30, 0.0)
        query = jnp.where(lane < HD, query, own).astype(BF16)

        def score(j, top):
            cols = pl.ds(pl.multiple_of(j * CK, CK), CK)
            s = lax.dot_general(
                query, kaug[cols, :], (((1,), (1,)), ((), ())),
                preferred_element_type=F32,
            )
            scores[:, cols] = s
            return jnp.maximum(top, fold(jnp.maximum, s))

        top = lax.fori_loop(j0, j1, score, jnp.full((TQ, 128), -jnp.inf, F32))
        top = jnp.max(top, axis=1, keepdims=True)

        def mix(j, carry):
            total, acc = carry
            cols = pl.ds(pl.multiple_of(j * CK, CK), CK)
            e = jnp.exp2((scores[:, cols] - top) * SCALE)
            total = total + fold(jnp.add, e)
            acc = acc + jnp.dot(
                e.astype(BF16), qkv_ref[cols, :], preferred_element_type=F32
            )
            return total, acc

        total, acc = lax.fori_loop(
            j0, j1, mix, (jnp.zeros((TQ, 128), F32), jnp.zeros((TQ, PACK), F32))
        )
        out = acc / jnp.sum(total, axis=1, keepdims=True)
        out = out.T.astype(BF16)
        o_ref[0:48, rows] = out[80:128]
        o_ref[48:80, rows] = out[208:240]


def attend(ids, qkv):
    return pl.pallas_call(
        attend_kernel,
        out_shape=jax.ShapeDtypeStruct((HD, SEQ), BF16),
        in_specs=[pl.BlockSpec(memory_space=pltpu.VMEM)] * 2,
        out_specs=pl.BlockSpec(memory_space=pltpu.VMEM),
        scratch_shapes=[
            pltpu.VMEM((SEQ, 128), BF16),
            pltpu.VMEM((TQ, SEQ), F32),
        ],
        compiler_params=pltpu.CompilerParams(vmem_limit_bytes=40 << 20),
        name="attend",
    )(ids, qkv)


def output_kernel(o_ref, wg_ref, out_ref, held, whole, ssem, rsem):
    dp, me = lax.axis_index("dp"), lax.axis_index("seq")
    barrier = pltpu.get_barrier_semaphore()
    for k in range(1, 16):
        to = (dp, lax.rem(me + k, 16))
        pl.semaphore_signal(barrier, inc=1, device_id=to, device_id_type=MESH)
    pl.semaphore_wait(barrier, 15)

    def mine(k):
        cols = pl.ds(pl.multiple_of(lax.rem(me + k, 16) * ROWS, ROWS), ROWS)
        return o_ref.at[:, cols]

    def slot(s):
        return held.at[pl.ds(pl.multiple_of(s * HD, 16), HD), :]

    copies = []
    for k in range(1, 16):
        cp = pltpu.make_async_remote_copy(
            src_ref=mine(k),
            dst_ref=slot(me),
            send_sem=ssem.at[k],
            recv_sem=rsem.at[k],
            device_id=(dp, lax.rem(me + k, 16)),
            device_id_type=MESH,
        )
        cp.start()
        copies.append(cp)
    own = pltpu.make_async_copy(mine(0), slot(me), ssem.at[0])
    own.start()
    for d in range(16):
        whole[:, d * HD : (d + 1) * HD] = wg_ref[d]
    own.wait()
    for k in range(1, 16):
        frm = slot(lax.rem(me + 16 - k, 16))
        pltpu.make_async_remote_copy(
            src_ref=frm,
            dst_ref=frm,
            send_sem=ssem.at[k],
            recv_sem=rsem.at[k],
            device_id=(dp, lax.rem(me + k, 16)),
            device_id_type=MESH,
        ).wait_recv()
    out_ref[...] = lax.dot_general(
        held[...], whole[...], (((0,), (0,)), ((), ())), preferred_element_type=F32
    ).astype(BF16)
    for cp in copies:
        cp.wait_send()


def output(o, wg):
    return pl.pallas_call(
        output_kernel,
        out_shape=jax.ShapeDtypeStruct((ROWS, D), BF16),
        in_specs=[pl.BlockSpec(memory_space=pltpu.VMEM)] * 2,
        out_specs=pl.BlockSpec(memory_space=pltpu.VMEM),
        scratch_shapes=[
            pltpu.VMEM((D, ROWS), BF16),
            pltpu.VMEM((D, D), BF16),
            pltpu.SemaphoreType.DMA((16,)),
            pltpu.SemaphoreType.DMA((16,)),
        ],
        compiler_params=pltpu.CompilerParams(
            collective_id=1, has_side_effects=True, vmem_limit_bytes=40 << 20
        ),
        name="output",
    )(o, wg)


def shards(patches, image_ids, w_qkv, w_out):
    q, k, v = w_qkv[0], w_qkv[1], w_qkv[2]
    spare = jnp.zeros((HD, PACK - 3 * HD), BF16)
    w = jnp.concatenate([q, v[:, :48], k, v[:, 48:], spare], axis=1)
    wg = lax.all_gather(w_out, ("dp", "seq"), axis=0, tiled=True)
    qkv = project(patches[0], w)
    o = attend(image_ids.reshape(SEQ // 128, 128), qkv)
    out = output(o, wg.reshape(16, D, HD))
    return out[None]


def solution(mesh):
    return jax.shard_map(
        shards,
        mesh=mesh,
        in_specs=(P("dp", "seq", None), P("dp", None), P(None, "dp", "seq"), P("seq", "dp")),
        out_specs=P("dp", "seq", None),
        check_vma=False,
    )
```

time: 312 us -> 455 us (1.46)
  waiting for transfers between devices: 127 us -> 330 us
  Pallas kernels: 0 us -> 105 us
  blocking collectives: 98.1 us -> 0 us
  matrix products: 47.2 us -> 0 us
  other arithmetic: 12.5 us -> 0 us
  loops' own time: 5.35 us -> 0 us
    all_gather x1, waiting for transfers between devices: 0.01 us -> 330 us  [shards(): wg = lax.all_gather(w_out, ('dp', 'seq'), axis=0, tiled=True)]
    reduce_scatter x1 -> x0, waiting for transfers between devices: 126 us -> none  [shards(): lax.psum_scatter(jnp.dot(heads_out, out_rows, preferred_element_type=jnp....]
    pallas_call x0 -> x3, Pallas kernels: none -> 105 us  [the longest x1 49.7 us: project(): pl.pallas_call(project_kernel, out_shape=jax.ShapeDtypeStruct((SEQ, PACK)...]
    all_gather x2 -> x0, blocking collectives: 98.1 us -> none  [the longest x1 54.6 us: shards(): lax.all_gather(w_qkv, 'dp', axis=1, tiled=True)]
    dot_general x18 -> x0, matrix products: 47.2 us -> none  [the longest x8 16.5 us: one_block(): jnp.einsum('hqk,khd->qhd', probs, vh, preferred_element_type=jnp.float32)]
    reduce_sum x8 -> x0, other arithmetic: 10.3 us -> none  [one_block(): probs = (expd / jnp.sum(expd, axis=-1, keepdims=True)).astype(jnp.bfloat16)]
    dynamic_slice x16 -> x0, local copies, waits for them, and re-layouts: 5.52 us -> none  [the longest x8 4.9 us: attend(): blocks = lax.map(one_block, jnp.arange(total // block, dtype=jnp.int32))]
    another operation x1 -> x0, loops' own time: 5.35 us -> none  [attend(): blocks = lax.map(one_block, jnp.arange(total // block, dtype=jnp.int32))]
  transfers between devices with their start and end apart: 2 -> 1, of which waited for: 1 -> 1; matrix products, arithmetic and copies ran while one was open for 1% -> 0% of each run, Pallas kernels for 0% -> 20%
where the time goes in v1:
time: 455 us
  waiting for transfers between devices  330 us (73%)
  Pallas kernels  105 us (23%)
  between operations  13.4 us (3%)
  local copies, waits for them, and re-layouts  6.08 us (1%)
    all_gather x1, waiting for transfers between devices, shards(): wg = lax.all_gather(w_out, ('dp', 'seq'), axis=0, tiled=True)  330 us
    pallas_call x1, Pallas kernels, project(): pl.pallas_call(project_kernel, out_shape=jax.ShapeDtypeStruct((SEQ, PACK)...  49.7 us
    pallas_call x1, Pallas kernels, attend(): pl.pallas_call(attend_kernel, out_shape=jax.ShapeDtypeStruct((HD, SEQ), B...  40.2 us
    pallas_call x1, Pallas kernels, output(): pl.pallas_call(output_kernel, out_shape=jax.ShapeDtypeStruct((ROWS, D), B...  15.1 us
  transfers between devices with their start and end apart: 1, of which 1 were waited for; matrix products, arithmetic and copies ran while one was open for 0% of the time, Pallas kernels for 20%

profile of v1, /device:TPU:1, one launch (start us, length us, event | category | flops | bytes accessed | tf_op | source)
XLA Modules:
  0.0 455.0 jit_solution(10394954209344713472)
XLA Ops:
  6.5 0.0 all-gather.2.cloned.1.call-start
  6.5 0.7 all-gather.2.cloned.1.call-update
  7.3 0.8 slice_bitcast_fusion
  8.0 0.1 slice.21
  8.1 0.1 concatenate.3.w_ref
  8.2 0.0 copy-start.1
  8.2 1.1 copy-done.1
  9.3 49.7 %project.1.qkv_ref = bf16[4096,256]{1,0:T(8,128)(2,1)S(1)} custom-call(bf16[256,1280]{1,0:T(8,128)(2,1)S(1)} %bitcast.13, bf16[80,256]{1,0:T(8,128)(2,1)S(1)} %concatenate.3.w_ref), custom_call_target="tpu_custom_call" | custom-call | tf_op jit(solution)/shard_map/project/pallas_call | solution.py:192
  59.0 0.0 copy-start.2
  59.0 0.7 copy-done.2
  59.7 40.2 %attend.1.o_ref = bf16[80,4096]{1,0:T(8,128)(2,1)S(1)} custom-call(s32[32,128]{1,0:T(8,128)S(1)} %bitcast.14, bf16[4096,256]{1,0:T(8,128)(2,1)S(1)} %project.1.qkv_ref), custom_call_target="tpu_custom_call" | custom-call | tf_op jit(solution)/shard_map/attend/pallas_call | solution.py:291
  100.0 329.8 %all-gather.2.cloned.1.call-done = bf16[20480,80]{1,0:T(8,128)(2,1)} async-done(((bf16[80,80]{1,0:T(8,128)(2,1)}), bf16[20480,80]{1,0:T(8,128)(2,1)}) %all-gather.2.cloned.1.call-update) | async-done | bytes 3276816 | tf_op jit(solution)/shard_map/all_gather | solution.py:377
  429.7 0.0 copy-start
  429.7 2.5 copy-done
  432.2 15.1 %output.1 = bf16[256,1280]{1,0:T(8,128)(2,1)S(1)} custom-call(bf16[80,4096]{1,0:T(8,128)(2,1)S(1)} %attend.1.o_ref, bf16[16,1280,80]{2,1,0:T(8,128)(2,1)S(1)} %bitcast.11), custom_call_target="tpu_custom_call" | custom-call | tf_op jit(solution)/shard_map/output/pallas_call | solution.py:355
  447.3 0.8 copy.6
  (1 shorter events, 0.0 us)
Async XLA Ops:
  6.5 423.2 %all-gather.2.cloned.1.call-start = ((), (), s32[]{:S(2)}) async-start(), calls=%async_computation | async-start | bytes 5263360 | tf_op jit(solution)/shard_map/all_gather | solution.py:377
  8.2 1.1 copy-start.1
  59.0 0.7 copy-start.2
  429.7 2.5 copy-start
Sparse Core Ops, SparseCore 0:
  9.2 420.4 all-gather.1

commit v2 on v1

--- a/solution.py
+++ b/solution.py
@@ -1,4 +1,4 @@
-import functools
+import itertools
 import math
 
 import jax
@@ -30,25 +30,29 @@
     return (lax.div(z, 2) * 4 + x, lax.rem(z, 2) * 8 + y * 2 + c)
 
 
-def project_kernel(x_ref, w_ref, qkv_ref, xbuf, wbuf, pbuf, ssem, rsem, lsem):
+def project_kernel(
+    x_ref, w_ref, qkv_ref, wo_ref, xbuf, wbuf, pbuf, zbuf, pack, ssem, rsem, lsem
+):
     x, y, z, c = place()
     zl = lax.rem(z, 2)
     xp, xm, x2 = lax.rem(x + 1, 4), lax.rem(x + 3, 4), lax.rem(x + 2, 4)
     yp, ym, y2 = lax.rem(y + 1, 4), lax.rem(y + 3, 4), lax.rem(y + 2, 4)
-    zp, zm = lax.rem(z + 1, 8), lax.rem(z + 7, 8)
     co = 1 - c
     mate = z + 1 - 2 * zl
-    to_xp, to_xm = device(xp, y, z, c), device(xm, y, z, c)
-    to_yp, to_ym = device(x, yp, z, c), device(x, ym, z, c)
-    to_zp, to_zm = device(x, y, zp, c), device(x, y, zm, c)
+    to_x = [device(xx, y, z, c) for xx in (xp, xm, x2)]
+    to_y = [device(x, yy, z, c) for yy in (yp, ym, y2)]
+    to_z = {d: device(x, y, lax.rem(z + d, 8), c) for d in range(1, 8)}
     to_co, to_mate = device(x, y, z, co), device(x, y, mate, c)
 
     barrier = pltpu.get_barrier_semaphore()
-    for to in (to_xp, to_xm, to_yp, to_ym, to_zp, to_zm, to_co):
+    for to in (*to_x, *to_y, *to_z.values(), to_co):
         pl.semaphore_signal(barrier, inc=1, device_id=to, device_id_type=MESH)
-    pl.semaphore_wait(barrier, 7)
-
-    sent = []
+    pl.semaphore_wait(barrier, 14)
+
+    sent, names, local = [], {}, []
+
+    def sem(*name):
+        return names.setdefault(name, len(names))
 
     def copy(src, dst, k, to):
         return pltpu.make_async_remote_copy(
@@ -60,130 +64,153 @@
             device_id_type=MESH,
         )
 
-    def send(src, dst, k, to):
-        cp = copy(src, dst, k, to)
+    def send(src, dst, to, *name):
+        cp = copy(src, dst, sem(*name), to)
         cp.start()
         sent.append(cp)
 
-    def arrived(dst, k):
-        copy(dst, dst, k, to_co).wait_recv()
+    def arrived(dst, *name):
+        copy(dst, dst, sem(*name), to_co).wait_recv()
+
+    def keep(src, dst):
+        cp = pltpu.make_async_copy(src, dst, lsem.at[len(local)])
+        cp.start()
+        local.append(cp)
+        return cp
+
+    def behind(d):
+        return lax.rem(z + 8 - d, 8)
 
     def wslot(zz, xx):
         row = pl.multiple_of((lax.div(zz, 2) * 4 + xx) * HD, 16)
         return wbuf.at[lax.rem(zz, 2), pl.ds(row, HD), :]
 
-    def zslot(j):
-        return lax.rem(z + 8 - j, 8) if j <= 4 else lax.rem(z + j - 4, 8)
-
-    def xid(j, k):
-        return 7 + 3 * j + k
-
     half = ROWS // 2
 
     def xpart(cc, yy, part):
         return xbuf.at[cc, yy, pl.ds(part * half, half), :]
 
-    send(w_ref, wslot(z, x), 0, to_zp)
-    send(w_ref, wslot(z, x), 4, to_zm)
-    send(w_ref, wslot(z, x), xid(0, 0), to_xp)
-    send(w_ref, wslot(z, x), xid(0, 1), to_xm)
+    w_mine, wo_mine = w_ref.at[:, 0:PACK], w_ref.at[:, PACK : PACK + 128]
+    for d in (1, 7, 3, 5, 2, 6, 4):
+        send(w_mine, wslot(z, x), to_z[d], "wz", d)
+    for to, k in zip(to_x, range(3)):
+        send(w_mine, wslot(z, x), to, "wx", 0, k)
+    for d in (1, 7, 2, 6, 3, 5, 4):
+        send(wo_mine, zbuf.at[z], to_z[d], "oz", d)
     for part in (0, 1):
         src = x_ref.at[pl.ds(part * half, half), :]
-        send(src, xpart(c, y, part), 31 + part, to_yp)
+        send(src, xpart(c, y, part), to_y[0], "y+", part)
         src = x_ref.at[pl.ds((1 - part) * half, half), :]
-        send(src, xpart(c, y, 1 - part), 34 - part, to_ym)
-    send(x_ref, xbuf.at[c, y], 37, to_co)
-    own_w = pltpu.make_async_copy(w_ref, wslot(z, x), lsem.at[8])
-    own_w.start()
-    own_x = pltpu.make_async_copy(x_ref, xbuf.at[c, y], lsem.at[9])
-    own_x.start()
-
-    def x_forward(j):
-        zz = zslot(j)
-        if j % 2 == 0:
-            arrived(wslot(zz, xm), xid(j, 0))
-            send(wslot(zz, xm), wslot(zz, xm), xid(j, 2), to_xp)
+        send(src, xpart(c, y, 1 - part), to_y[1], "y-", 1 - part)
+    send(x_ref, xbuf.at[c, y], to_co, "c", 0)
+    own_x = keep(x_ref, xbuf.at[c, y])
+    own_w = keep(w_mine, wslot(z, x))
+    own_o = keep(wo_mine, zbuf.at[z])
+
+    for d in (1, 7, 3, 5, 2, 6, 4):
+        here = wslot(behind(d), x)
+        arrived(here, "wz", d)
+        for to, k in zip(to_x, range(3)):
+            send(here, here, to, "wx", d, k)
+
+    for d in range(1, 8):
+        arrived(zbuf.at[behind(d)], "oz", d)
+    own_o.wait()
+    for zz in range(8):
+        lane = (zz % 2) * 4 * HD + (zz // 2) * HD
+        pack[:, lane : lane + HD] = zbuf[zz][:, :HD]
+    for to, k in zip(to_y, range(3)):
+        send(pack, wo_ref.at[c, x, y], to, "oy", k)
+    own_pack = keep(pack, wo_ref.at[c, x, y])
+
+    arrived(xpart(c, ym, 0), "y+", 0)
+    send(xpart(c, ym, 0), xpart(c, ym, 0), to_y[0], "y2", 0)
+    arrived(xpart(c, yp, 1), "y-", 1)
+    send(xpart(c, yp, 1), xpart(c, yp, 1), to_y[1], "y2", 1)
+
+    def w_here(ds):
+        for d in ds:
+            for k, xx in enumerate((xm, xp, x2)):
+                arrived(wslot(behind(d), xx), "wx", d, k)
+
+    def block(lo, cc, yy):
+        row = pl.multiple_of((lo * 8 + yy * 2 + cc) * ROWS, ROWS)
+        return qkv_ref.at[pl.ds(row, ROWS), :]
+
+    places = ((c, y), (co, y), (c, ym), (c, yp), (co, ym), (co, yp), (c, y2), (co, y2))
+
+    def project(i, whose):
+        head = zl if whose else 1 - zl
+        cc, yy = places[i]
+        pbuf[i, whose] = jnp.dot(
+            xbuf[cc, yy], wbuf[head], preferred_element_type=F32
+        ).astype(BF16)
+        if whose:
+            keep(pbuf.at[i, 1], block(zl, cc, yy))
         else:
-            arrived(wslot(zz, xp), xid(j, 1))
-            send(wslot(zz, xp), wslot(zz, xp), xid(j, 2), to_xm)
-
-    before = 0
-    for j in (1, 5, 2, 6, 3, 7, 4):
-        here = wslot(zslot(j), x)
-        arrived(here, j - 1)
-        if j in (1, 2, 3):
-            send(here, here, j, to_zp)
-        if j in (5, 6):
-            send(here, here, j, to_zm)
-        send(here, here, xid(j, 0), to_xp)
-        send(here, here, xid(j, 1), to_xm)
-        x_forward(before)
-        before = j
-    x_forward(before)
-
-    arrived(xpart(c, ym, 0), 31)
-    send(xpart(c, ym, 0), xpart(c, ym, 0), 35, to_yp)
-    arrived(xpart(c, yp, 1), 34)
-    send(xpart(c, yp, 1), xpart(c, yp, 1), 36, to_ym)
-
-    for j in range(8):
-        zz = zslot(j)
-        if j % 2 == 0:
-            arrived(wslot(zz, xp), xid(j, 1))
-        else:
-            arrived(wslot(zz, xm), xid(j, 0))
-        arrived(wslot(zz, x2), xid(j, 2))
+            send(pbuf.at[i, 0], block(zl, cc, yy), to_mate, "mate", i)
+
+    w_here((1, 7, 3, 5))
+    own_x.wait()
+    project(0, 0)
+    arrived(xbuf.at[co, y], "c", 0)
+    project(1, 0)
     own_w.wait()
-
-    kept = []
-
-    def block(cc, yy):
-        source = zl * 8 + yy * 2 + cc
-        return qkv_ref.at[pl.ds(pl.multiple_of(source * ROWS, ROWS), ROWS), :]
-
-    def project(i, cc, yy):
-        patches = xbuf[cc, yy]
-        for whose, head in ((0, 1 - zl), (1, zl)):
-            pbuf[i, whose] = jnp.dot(
-                patches, wbuf[head], preferred_element_type=F32
-            ).astype(BF16)
-            if whose == 0:
-                send(pbuf.at[i, 0], block(cc, yy), 41 + i, to_mate)
-            else:
-                keep = pltpu.make_async_copy(pbuf.at[i, 1], block(cc, yy), lsem.at[i])
-                keep.start()
-                kept.append(keep)
-
-    own_x.wait()
-    project(0, c, y)
-    arrived(xbuf.at[co, y], 37)
-    project(1, co, y)
-    arrived(xpart(c, ym, 1), 32)
-    send(xbuf.at[c, ym], xbuf.at[c, ym], 38, to_co)
-    arrived(xpart(c, yp, 0), 33)
-    send(xbuf.at[c, yp], xbuf.at[c, yp], 39, to_co)
-    project(2, c, ym)
-    project(3, c, yp)
-    arrived(xbuf.at[co, ym], 38)
-    project(4, co, ym)
-    arrived(xbuf.at[co, yp], 39)
-    project(5, co, yp)
-    arrived(xpart(c, y2, 0), 35)
-    arrived(xpart(c, y2, 1), 36)
-    send(xbuf.at[c, y2], xbuf.at[c, y2], 40, to_co)
-    project(6, c, y2)
-    arrived(xbuf.at[co, y2], 40)
-    project(7, co, y2)
-
-    theirs = 1 - zl
-    for i, (cc, yy) in enumerate(
-        ((c, y), (co, y), (c, ym), (c, yp), (co, ym), (co, yp), (c, y2), (co, y2))
-    ):
-        source = theirs * 8 + yy * 2 + cc
-        dst = qkv_ref.at[pl.ds(pl.multiple_of(source * ROWS, ROWS), ROWS), :]
-        arrived(dst, 41 + i)
-    for keep in kept:
-        keep.wait()
+    w_here((0, 2, 6, 4))
+    project(0, 1)
+    project(1, 1)
+
+    own_pack.wait()
+    for k, yy in enumerate((y, ym, yp, y2)):
+        here = wo_ref.at[c, x, yy]
+        if k:
+            arrived(here, "oy", k - 1)
+        send(here, here, to_x[0], "ox", k, 0)
+        send(here, here, to_x[1], "ox", k, 1)
+
+    arrived(xpart(c, ym, 1), "y+", 1)
+    send(xbuf.at[c, ym], xbuf.at[c, ym], to_co, "c", 1)
+    arrived(xpart(c, yp, 0), "y-", 0)
+    send(xbuf.at[c, yp], xbuf.at[c, yp], to_co, "c", 2)
+    project(2, 0)
+    project(3, 0)
+    arrived(xbuf.at[co, ym], "c", 1)
+    project(4, 0)
+    arrived(xbuf.at[co, yp], "c", 2)
+    project(5, 0)
+    for i in (2, 3, 4, 5):
+        project(i, 1)
+
+    for k, yy in enumerate((y, ym, yp, y2)):
+        side = k % 2
+        here = wo_ref.at[c, (xm, xp)[side], yy]
+        arrived(here, "ox", k, side)
+        send(here, here, to_x[side], "ox", k, 2)
+
+    arrived(xpart(c, y2, 0), "y2", 0)
+    arrived(xpart(c, y2, 1), "y2", 1)
+    send(xbuf.at[c, y2], xbuf.at[c, y2], to_co, "c", 3)
+    project(6, 0)
+    arrived(xbuf.at[co, y2], "c", 3)
+    project(7, 0)
+    project(6, 1)
+    project(7, 1)
+
+    send(wo_ref.at[c, x], wo_ref.at[c, x], to_co, "oc", 0)
+    for k, yy in enumerate((y, ym, yp, y2)):
+        side = 1 - k % 2
+        arrived(wo_ref.at[c, (xm, xp)[side], yy], "ox", k, side)
+    send(wo_ref.at[c, xm], wo_ref.at[c, xm], to_co, "oc", 1)
+    send(wo_ref.at[c, xp], wo_ref.at[c, xp], to_co, "oc", 2)
+    for k, yy in enumerate((y, ym, yp, y2)):
+        arrived(wo_ref.at[c, x2, yy], "ox", k, 2)
+    send(wo_ref.at[c, x2], wo_ref.at[c, x2], to_co, "oc", 3)
+    for i, (cc, yy) in enumerate(places):
+        arrived(block(1 - zl, cc, yy), "mate", i)
+    for k, xx in enumerate((x, xm, xp, x2)):
+        arrived(wo_ref.at[co, xx], "oc", k)
+    for cp in local[4:]:
+        cp.wait()
     for cp in sent:
         cp.wait_send()
 
@@ -191,19 +218,24 @@
 def project(patches, w):
     return pl.pallas_call(
         project_kernel,
-        out_shape=jax.ShapeDtypeStruct((SEQ, PACK), BF16),
+        out_shape=(
+            jax.ShapeDtypeStruct((SEQ, PACK), BF16),
+            jax.ShapeDtypeStruct((2, 4, 4, HD, 8 * HD), BF16),
+        ),
         in_specs=[
             pl.BlockSpec(memory_space=pl.ANY),
             pl.BlockSpec(memory_space=pltpu.VMEM),
         ],
-        out_specs=pl.BlockSpec(memory_space=pl.ANY),
+        out_specs=(pl.BlockSpec(memory_space=pl.ANY),) * 2,
         scratch_shapes=[
             pltpu.VMEM((2, 4, ROWS, D), BF16),
             pltpu.VMEM((2, D, PACK), BF16),
             pltpu.VMEM((8, 2, ROWS, PACK), BF16),
-            pltpu.SemaphoreType.DMA((49,)),
-            pltpu.SemaphoreType.DMA((49,)),
-            pltpu.SemaphoreType.DMA((10,)),
+            pltpu.VMEM((8, HD, 128), BF16),
+            pltpu.VMEM((HD, 8 * HD), BF16),
+            pltpu.SemaphoreType.DMA((80,)),
+            pltpu.SemaphoreType.DMA((80,)),
+            pltpu.SemaphoreType.DMA((16,)),
         ],
         compiler_params=pltpu.CompilerParams(
             collective_id=0, has_side_effects=True, vmem_limit_bytes=40 << 20
@@ -331,8 +363,16 @@
         copies.append(cp)
     own = pltpu.make_async_copy(mine(0), slot(me), ssem.at[0])
     own.start()
-    for d in range(16):
-        whole[:, d * HD : (d + 1) * HD] = wg_ref[d]
+
+    @pl.loop(0, 8)
+    def _(i):
+        for zl, x, zh in itertools.product(range(2), range(4), range(4)):
+            row = pl.multiple_of((zl * 8 + i) * HD, 16)
+            col, lane = (zh * 4 + x) * HD, (zl * 4 + zh) * HD
+            whole[pl.ds(row, HD), col : col + HD] = wg_ref[
+                lax.rem(i, 2), x, lax.div(i, 2), :, lane : lane + HD
+            ]
+
     own.wait()
     for k in range(1, 16):
         frm = slot(lax.rem(me + 16 - k, 16))
@@ -373,11 +413,11 @@
 def shards(patches, image_ids, w_qkv, w_out):
     q, k, v = w_qkv[0], w_qkv[1], w_qkv[2]
     spare = jnp.zeros((HD, PACK - 3 * HD), BF16)
-    w = jnp.concatenate([q, v[:, :48], k, v[:, 48:], spare], axis=1)
-    wg = lax.all_gather(w_out, ("dp", "seq"), axis=0, tiled=True)
-    qkv = project(patches[0], w)
+    more = jnp.zeros((HD, 128 - HD), BF16)
+    w = jnp.concatenate([q, v[:, :48], k, v[:, 48:], spare, w_out, more], axis=1)
+    qkv, wo = project(patches[0], w)
     o = attend(image_ids.reshape(SEQ // 128, 128), qkv)
-    out = output(o, wg.reshape(16, D, HD))
+    out = output(o, wo)
     return out[None]
 
 

time: 455 us -> 113 us (0.25)
  waiting for transfers between devices: 330 us -> 0 us
  between operations: 13.4 us -> 0.06 us
    all_gather x1 -> x0, waiting for transfers between devices: 330 us -> none  [shards(): wg = lax.all_gather(w_out, ('dp', 'seq'), axis=0, tiled=True)]
  transfers between devices with their start and end apart: 1 -> 0, of which waited for: 1 -> 0; matrix products, arithmetic and copies ran while one was open for 0% -> 0% of each run, Pallas kernels for 20% -> 0%
where the time goes in v2:
time: 113 us
  Pallas kernels  108 us (96%)
  local copies, waits for them, and re-layouts  4.33 us (4%)
    pallas_call x1, Pallas kernels, project(): pl.pallas_call(project_kernel, out_shape=(jax.ShapeDtypeStruct((SEQ, PACK...  48.9 us
    pallas_call x1, Pallas kernels, attend(): pl.pallas_call(attend_kernel, out_shape=jax.ShapeDtypeStruct((HD, SEQ), B...  44.8 us
    pallas_call x1, Pallas kernels, output(): pl.pallas_call(output_kernel, out_shape=jax.ShapeDtypeStruct((ROWS, D), B...  14.5 us
    unnamed x5, local copies, waits for them, and re-layouts  2.63 us

profile of v2, /device:TPU:1, one launch (start us, length us, event | category | flops | bytes accessed | tf_op | source)
XLA Modules:
  0.0 112.6 jit_solution(161019503135379718)
XLA Ops:
  0.0 0.8 slice_bitcast_fusion
  0.8 0.1 slice.21
  0.9 0.8 concatenate.3.w_ref
  1.7 0.0 copy-start
  1.7 1.1 copy-done
  2.8 48.9 %project.1 = (bf16[4096,256]{1,0:T(8,128)(2,1)S(1)}, bf16[2,4,4,80,640]{4,3,2,1,0:T(8,128)(2,1)S(1)}) custom-call(bf16[256,1280]{1,0:T(8,128)(2,1)S(1)} %bitcast.11, bf16[80,384]{1,0:T(8,128)(2,1)S(1)} %concatenate.3.w_ref), custom_call_target="tpu_custom_call" | custom-call | tf_op jit(solution)/shard_map/project/pallas_call | solution.py:219
  51.8 0.0 copy-start.1
  51.8 0.7 copy-done.1
  52.5 44.8 %attend.1.o_ref = bf16[80,4096]{1,0:T(8,128)(2,1)S(1)} custom-call(s32[32,128]{1,0:T(8,128)S(1)} %bitcast.12, bf16[4096,256]{1,0:T(8,128)(2,1)S(1)} %get-tuple-element.7.qkv_ref), custom_call_target="tpu_custom_call" | custom-call | tf_op jit(solution)/shard_map/attend/pallas_call | solution.py:323
  97.3 14.5 %output.1 = bf16[256,1280]{1,0:T(8,128)(2,1)S(1)} custom-call(bf16[80,4096]{1,0:T(8,128)(2,1)S(1)} %attend.1.o_ref, bf16[2,4,4,80,640]{4,3,2,1,0:T(8,128)(2,1)S(1)} %get-tuple-element.8.wg_ref), custom_call_target="tpu_custom_call" | custom-call | tf_op jit(solution)/shard_map/output/pallas_call | solution.py:395
  111.8 0.8 copy.6
  (2 shorter events, 0.0 us)
Async XLA Ops:
  1.7 1.1 copy-start
  51.8 0.7 copy-start.1

commit v3 on v2

--- a/solution.py
+++ b/solution.py
@@ -1,3 +1,4 @@
+import functools
 import itertools
 import math
 
@@ -245,89 +246,128 @@
 
 
 TQ = 256
-CK = 512
+CK = 768
+SUB = 128
+BLOCKS = SEQ // TQ
 SCALE = math.log2(math.e) / math.sqrt(HD)
 
 
-def fold(op, a):
-    parts = [a[:, i : i + 128] for i in range(0, a.shape[1], 128)]
+def rows_fold(op, a):
+    parts = [a[i : i + 8] for i in range(0, a.shape[0], 8)]
     while len(parts) > 1:
-        parts = [op(parts[i], parts[i + 1]) for i in range(0, len(parts), 2)]
+        odd = parts[len(parts) // 2 * 2 :]
+        parts = [op(l, r) for l, r in zip(parts[::2], parts[1::2])] + odd
     return parts[0]
 
 
-def attend_kernel(ids_ref, qkv_ref, o_ref, kaug, scores):
+def attend_kernel(
+    ids_ref, qkv_ref, o_ref, kaug, qaug, vt, s0, s1, e0, e1, acc, state
+):
     ids = ids_ref[...]
-    cuts = [
-        jnp.sum((ids < a).astype(F32)).astype(jnp.int32) for a in (1, 2, 3)
-    ]
-
-    def image_of(start, rows):
-        pos = lax.broadcasted_iota(jnp.int32, (rows, 128), 0) + start
+    cuts = [jnp.sum((ids < a).astype(F32)).astype(jnp.int32) for a in (1, 2, 3)]
+
+    def image_of(pos):
         return sum((pos >= cut).astype(jnp.int32) for cut in cuts)
 
     lane = lax.broadcasted_iota(jnp.int32, (TQ, 128), 1)
-
-    @pl.loop(0, SEQ // TQ)
+    kpos = lax.broadcasted_iota(jnp.int32, (TQ, 128), 0)
+    mark = lax.broadcasted_iota(jnp.int32, (128 - HD, TQ), 0)
+    qpos = lax.broadcasted_iota(jnp.int32, (128 - HD, TQ), 1)
+
+    @pl.loop(0, BLOCKS)
     def _(i):
         rows = pl.ds(pl.multiple_of(i * TQ, TQ), TQ)
-        keys = qkv_ref[rows, 128:256].astype(F32)
-        other = jnp.where(image_of(i * TQ, TQ) != lane - HD, 1.0, 0.0)
-        kaug[rows, :] = jnp.where(lane < HD, keys, other).astype(BF16)
-
-    @pl.loop(0, SEQ // TQ)
-    def _(i):
+        other = image_of(kpos + i * TQ) != lane - HD
+        kaug[rows, :] = jnp.where(
+            lane < HD, qkv_ref[rows, 128:256], jnp.where(other, 1.0, 0.0).astype(BF16)
+        )
+        turned = qkv_ref[rows, :].T
+        own = image_of(qpos + i * TQ) == mark
+        qaug[0:HD, rows] = turned[0:HD]
+        qaug[HD:128, rows] = jnp.where(own, -1e30, 0.0).astype(BF16)
+        vt[0:48, rows] = turned[80:128]
+        vt[48:80, rows] = turned[208:240]
+
+    kaug[SEQ : SEQ + CK, :] = jnp.ones((CK, 128), BF16)
+    vt[:, SEQ : SEQ + CK] = jnp.zeros((HD, CK), BF16)
+    for ref in (s0, s1, e0, e1, acc, state):
+        ref[...] = jnp.zeros_like(ref)
+
+    def span(i):
         first = i * TQ
-        rows = pl.ds(pl.multiple_of(first, TQ), TQ)
         lo, hi = jnp.int32(0), jnp.int32(SEQ)
         for cut in cuts:
             lo = jnp.maximum(lo, jnp.where(cut <= first, cut, 0))
             hi = jnp.minimum(hi, jnp.where(cut >= first + TQ, cut, SEQ))
-        j0, j1 = lax.div(lo, CK), lax.div(hi + CK - 1, CK)
-        query = qkv_ref[rows, 0:128].astype(F32)
-        own = jnp.where(image_of(first, TQ) == lane - HD, -1e30, 0.0)
-        query = jnp.where(lane < HD, query, own).astype(BF16)
-
-        def score(j, top):
-            cols = pl.ds(pl.multiple_of(j * CK, CK), CK)
-            s = lax.dot_general(
-                query, kaug[cols, :], (((1,), (1,)), ((), ())),
-                preferred_element_type=F32,
-            )
-            scores[:, cols] = s
-            return jnp.maximum(top, fold(jnp.maximum, s))
-
-        top = lax.fori_loop(j0, j1, score, jnp.full((TQ, 128), -jnp.inf, F32))
-        top = jnp.max(top, axis=1, keepdims=True)
-
-        def mix(j, carry):
-            total, acc = carry
-            cols = pl.ds(pl.multiple_of(j * CK, CK), CK)
-            e = jnp.exp2((scores[:, cols] - top) * SCALE)
-            total = total + fold(jnp.add, e)
-            acc = acc + jnp.dot(
-                e.astype(BF16), qkv_ref[cols, :], preferred_element_type=F32
-            )
-            return total, acc
-
-        total, acc = lax.fori_loop(
-            j0, j1, mix, (jnp.zeros((TQ, 128), F32), jnp.zeros((TQ, PACK), F32))
+        lo = lax.div(lo, 128) * 128
+        return lo, lax.div(hi - lo + CK - 1, CK)
+
+    steps = lax.fori_loop(0, BLOCKS, lambda i, n: n + span(i)[1], jnp.int32(0))
+
+    def step(s_new, s_old, e_old, e_new, carry):
+        i1, k1, i2, k2, i3, k3, first2, first3 = carry
+        high, top = state[0:1, :], state[8:9, :]
+        rescale3, total = state[16:17, :], state[24:32, :]
+        before = jnp.where(first2 > 0, -jnp.inf, top)
+        top = jnp.maximum(before, high)
+        rescale2 = jnp.exp2((before - top) * SCALE)
+        block1 = jnp.minimum(i1, BLOCKS - 1)
+        query = qaug[:, pl.ds(pl.multiple_of(block1 * TQ, TQ), TQ)]
+        highs, sums = [], []
+        for u in range(0, CK, SUB):
+            part = slice(u, u + SUB)
+            keys = kaug[pl.ds(pl.multiple_of(k1 + u, 128), SUB), :]
+            s = jnp.dot(keys, query, preferred_element_type=F32)
+            s_new[part, :] = s
+            highs.append(rows_fold(jnp.maximum, s))
+            e = jnp.exp2((s_old[part, :] - top) * SCALE)
+            sums.append(rows_fold(jnp.add, e))
+            e_new[part, :] = e.astype(BF16)
+            if u == 0:
+                values = vt[:, pl.ds(pl.multiple_of(k3, 128), CK)]
+                mixed = jnp.dot(values, e_old[...], preferred_element_type=F32)
+        mixed = acc[...] * rescale3 + mixed
+        acc[...] = mixed
+        inverse = 1.0 / jnp.sum(total, axis=0, keepdims=True)
+        out = pl.ds(pl.multiple_of(i3 * TQ, TQ), TQ)
+        o_ref[:, out] = (mixed * inverse).astype(BF16)
+        state[0:1, :] = jnp.max(
+            functools.reduce(jnp.maximum, highs), axis=0, keepdims=True
         )
-        out = acc / jnp.sum(total, axis=1, keepdims=True)
-        out = out.T.astype(BF16)
-        o_ref[0:48, rows] = out[80:128]
-        o_ref[48:80, rows] = out[208:240]
+        state[8:9, :] = top
+        state[16:17, :] = rescale2
+        state[24:32, :] = total * rescale2 + functools.reduce(jnp.add, sums)
+        lo, n = span(block1)
+        first1 = jnp.where(k1 == lo, 1, 0)
+        last1 = jnp.where(k1 + CK >= lo + n * CK, 1, 0)
+        following = jnp.minimum(i1 + last1, BLOCKS)
+        start = span(jnp.minimum(following, BLOCKS - 1))[0]
+        k_next = jnp.where(last1 > 0, start, k1 + CK)
+        return following, k_next, i1, k1, i2, k2, first1, first2
+
+    def pair(_, carry):
+        carry = step(s0, s1, e0, e1, carry)
+        return step(s1, s0, e1, e0, carry)
+
+    lax.fori_loop(0, lax.div(steps + 3, 2), pair, (jnp.int32(0),) * 8)
 
 
 def attend(ids, qkv):
     return pl.pallas_call(
         attend_kernel,
-        out_shape=jax.ShapeDtypeStruct((HD, SEQ), BF16),
+        out_shape=jax.ShapeDtypeStruct((HD, SEQ + TQ), BF16),
         in_specs=[pl.BlockSpec(memory_space=pltpu.VMEM)] * 2,
         out_specs=pl.BlockSpec(memory_space=pltpu.VMEM),
         scratch_shapes=[
-            pltpu.VMEM((SEQ, 128), BF16),
-            pltpu.VMEM((TQ, SEQ), F32),
+            pltpu.VMEM((SEQ + CK, 128), BF16),
+            pltpu.VMEM((128, SEQ), BF16),
+            pltpu.VMEM((HD, SEQ + CK), BF16),
+            pltpu.VMEM((CK, TQ), F32),
+            pltpu.VMEM((CK, TQ), F32),
+            pltpu.VMEM((CK, TQ), BF16),
+            pltpu.VMEM((CK, TQ), BF16),
+            pltpu.VMEM((HD, TQ), F32),
+            pltpu.VMEM((32, TQ), F32),
         ],
         compiler_params=pltpu.CompilerParams(vmem_limit_bytes=40 << 20),
         name="attend",

time: 113 us -> 81.7 us (0.72)
  Pallas kernels: 108 us -> 77 us
    pallas_call x1, Pallas kernels: 44.8 us -> 13.6 us  [attend(): pl.pallas_call(attend_kernel, out_shape=jax.ShapeDtypeStruct((HD, SEQ + T...]
where the time goes in v3:
time: 81.7 us; the launch traced here: 81.4 us
  Pallas kernels  77 us (94%)
  local copies, waits for them, and re-layouts  4.33 us (5%)
    pallas_call x1, Pallas kernels, project(): pl.pallas_call(project_kernel, out_shape=(jax.ShapeDtypeStruct((SEQ, PACK...  48.9 us
    pallas_call x1, Pallas kernels, output(): pl.pallas_call(output_kernel, out_shape=jax.ShapeDtypeStruct((ROWS, D), B...  14.5 us
    pallas_call x1, Pallas kernels, attend(): pl.pallas_call(attend_kernel, out_shape=jax.ShapeDtypeStruct((HD, SEQ + T...  13.6 us
    unnamed x5, local copies, waits for them, and re-layouts  2.63 us

profile of v3, /device:TPU:1, one launch (start us, length us, event | category | flops | bytes accessed | tf_op | source)
XLA Modules:
  0.0 81.4 jit_solution(13767686997860630231)
XLA Ops:
  0.0 0.8 slice_bitcast_fusion
  0.8 0.1 slice.21
  0.9 0.8 %concatenate.3.w_ref = bf16[80,384]{1,0:T(8,128)(2,1)S(1)} concatenate(bf16[80,80]{1,0:T(8,128)(2,1)S(1)} %get-tuple-element.10, bf16[80,48]{1,0:T(8,128)(2,1)S(1)} %bitcast.13, bf16[80,80]{1,0:T(8,128)(2,1)S(1)} %get-tuple-element.9, bf16[80,32]{1,0:T(8,128)(2,1)S(1)} %slice.21, bf16[80,16]{1,0:T(8,128)(2,1)S(1)} %broadcast_in_dim.9, bf16[80,80]{1,0:T(8,128)(2,1)} %param.7, ...), dimensions={1} | concatenate | bytes 122880 | tf_op jit(solution)/shard_map/concatenate | solution.py:457
  1.7 0.0 copy-start
  1.7 1.1 %copy-done = bf16[1,256,1280]{2,1,0:T(8,128)(2,1)S(1)} copy-done((bf16[1,256,1280]{2,1,0:T(8,128)(2,1)S(1)}, bf16[1,256,1280]{2,1,0:T(8,128)(2,1)}, u32[]{:S(2)}) %copy-start) | copy-done | bytes 655384
  2.8 48.9 %project.1 = (bf16[4096,256]{1,0:T(8,128)(2,1)S(1)}, bf16[2,4,4,80,640]{4,3,2,1,0:T(8,128)(2,1)S(1)}) custom-call(bf16[256,1280]{1,0:T(8,128)(2,1)S(1)} %bitcast.11, bf16[80,384]{1,0:T(8,128)(2,1)S(1)} %concatenate.3.w_ref), custom_call_target="tpu_custom_call" | custom-call | tf_op jit(solution)/shard_map/project/pallas_call | solution.py:220
  51.8 0.0 copy-start.1
  51.8 0.7 copy-done.1
  52.5 13.6 %attend.1.o_ref = bf16[80,4352]{1,0:T(8,128)(2,1)S(1)} custom-call(s32[32,128]{1,0:T(8,128)S(1)} %bitcast.12, bf16[4096,256]{1,0:T(8,128)(2,1)S(1)} %get-tuple-element.7.qkv_ref), custom_call_target="tpu_custom_call" | custom-call | tf_op jit(solution)/shard_map/attend/pallas_call | solution.py:356
  66.1 14.5 %output.1 = bf16[256,1280]{1,0:T(8,128)(2,1)S(1)} custom-call(bf16[80,4352]{1,0:T(8,128)(2,1)S(1)} %attend.1.o_ref, bf16[2,4,4,80,640]{4,3,2,1,0:T(8,128)(2,1)S(1)} %get-tuple-element.8.wg_ref), custom_call_target="tpu_custom_call" | custom-call | tf_op jit(solution)/shard_map/output/pallas_call | solution.py:435
  80.6 0.8 %copy.6 = bf16[1,256,1280]{2,1,0:T(8,128)(2,1)} copy(bf16[1,256,1280]{2,1,0:T(8,128)(2,1)S(1)} %bitcast.10) | data formatting | bytes 1310720
  (2 shorter events, 0.0 us)
Async XLA Ops:
  1.7 1.1 %copy-start = (bf16[1,256,1280]{2,1,0:T(8,128)(2,1)S(1)}, bf16[1,256,1280]{2,1,0:T(8,128)(2,1)}, u32[]{:S(2)}) copy-start(bf16[1,256,1280]{2,1,0:T(8,128)(2,1)} %param.4) | copy-start | bytes 1966084
  51.8 0.7 copy-start.1

commit v4 on v3

--- a/solution.py
+++ b/solution.py
@@ -15,6 +15,11 @@
 ROWS = 256
 SEQ = 4096
 PACK = 256
+TQ = 256
+CK = 768
+SUB = 128
+BLOCKS = SEQ // TQ
+SCALE = math.log2(math.e) / math.sqrt(HD)
 BF16 = jnp.bfloat16
 F32 = jnp.float32
 
@@ -32,7 +37,9 @@
 
 
 def project_kernel(
-    x_ref, w_ref, qkv_ref, wo_ref, xbuf, wbuf, pbuf, zbuf, pack, ssem, rsem, lsem
+    x_ref, ids_ref, wqkv_ref, wout_ref,
+    kaug, qaug, vt, cut_ref, wo_ref,
+    ids, wq, wo, mine, xbuf, wbuf, pbuf, qkv, zbuf, pack, ssem, rsem, lsem,
 ):
     x, y, z, c = place()
     zl = lax.rem(z, 2)
@@ -48,7 +55,6 @@
     barrier = pltpu.get_barrier_semaphore()
     for to in (*to_x, *to_y, *to_z.values(), to_co):
         pl.semaphore_signal(barrier, inc=1, device_id=to, device_id_type=MESH)
-    pl.semaphore_wait(barrier, 14)
 
     sent, names, local = [], {}, []
 
@@ -79,47 +85,139 @@
         local.append(cp)
         return cp
 
+    loads = (
+        keep(wqkv_ref, wq), keep(wout_ref, wo), keep(x_ref, xbuf.at[c, y]),
+        keep(ids_ref, ids),
+    )
+    loads[0].wait()
+    loads[1].wait()
+    mine[:, 0:80] = wq[0]
+    mine[:, 80:128] = wq[2][:, :48]
+    mine[:, 128:208] = wq[1]
+    mine[:, 208:240] = wq[2][:, 48:]
+    mine[:, 240:256] = jnp.zeros((HD, 16), BF16)
+    mine[:, 256:336] = wo[...]
+    pl.semaphore_wait(barrier, 14)
+
     def behind(d):
         return lax.rem(z + 8 - d, 8)
 
-    def wslot(zz, xx):
+    def lanes(part):
+        return slice(0, PACK) if part is None else slice(part * 128, part * 128 + 128)
+
+    def wslot(zz, xx, part=None):
         row = pl.multiple_of((lax.div(zz, 2) * 4 + xx) * HD, 16)
-        return wbuf.at[lax.rem(zz, 2), pl.ds(row, HD), :]
+        return wbuf.at[lax.rem(zz, 2), pl.ds(row, HD), lanes(part)]
 
     half = ROWS // 2
 
     def xpart(cc, yy, part):
         return xbuf.at[cc, yy, pl.ds(part * half, half), :]
 
-    w_mine, wo_mine = w_ref.at[:, 0:PACK], w_ref.at[:, PACK : PACK + 128]
-    for d in (1, 7, 3, 5, 2, 6, 4):
-        send(w_mine, wslot(z, x), to_z[d], "wz", d)
-    for to, k in zip(to_x, range(3)):
-        send(w_mine, wslot(z, x), to, "wx", 0, k)
-    for d in (1, 7, 2, 6, 3, 5, 4):
-        send(wo_mine, zbuf.at[z], to_z[d], "oz", d)
+    theirs, ours = (1, 7, 3, 5), (2, 6, 4)
+    wo_mine = mine.at[:, PACK : PACK + 128]
+
+    def w_mine(part=None):
+        return mine.at[:, lanes(part)]
+
+    for part in (0, 1):
+        for d in theirs:
+            send(w_mine(part), wslot(z, x, part), to_z[d], "wz", d, part)
     for part in (0, 1):
         src = x_ref.at[pl.ds(part * half, half), :]
         send(src, xpart(c, y, part), to_y[0], "y+", part)
         src = x_ref.at[pl.ds((1 - part) * half, half), :]
         send(src, xpart(c, y, 1 - part), to_y[1], "y-", 1 - part)
     send(x_ref, xbuf.at[c, y], to_co, "c", 0)
-    own_x = keep(x_ref, xbuf.at[c, y])
-    own_w = keep(w_mine, wslot(z, x))
+    for d in ours:
+        send(w_mine(), wslot(z, x), to_z[d], "wz", d, None)
+    for d in (1, 7, 2, 6, 3, 5, 4):
+        send(wo_mine, zbuf.at[z], to_z[d], "oz", d)
+    own_w = keep(w_mine(), wslot(z, x))
     own_o = keep(wo_mine, zbuf.at[z])
 
-    for d in (1, 7, 3, 5, 2, 6, 4):
+    def along_x(src, d, part):
+        for to, k in zip(to_x, range(3)):
+            send(src, wslot(behind(d), x, part), to, "wx", d, part, k)
+
+    for part in (0, 1):
+        for d in theirs:
+            here = wslot(behind(d), x, part)
+            arrived(here, "wz", d, part)
+            along_x(here, d, part)
+    along_x(w_mine(), 0, None)
+    for d in ours:
         here = wslot(behind(d), x)
-        arrived(here, "wz", d)
-        for to, k in zip(to_x, range(3)):
-            send(here, here, to, "wx", d, k)
+        arrived(here, "wz", d, None)
+        along_x(here, d, None)
+
+    def w_here(ds, part):
+        for d in ds:
+            for k, xx in enumerate((xm, xp, x2)):
+                arrived(wslot(behind(d), xx, part), "wx", d, part, k)
+
+    places = ((c, y), (co, y), (c, ym), (c, yp), (co, ym), (co, yp), (c, y2), (co, y2))
+
+    def block(lo, i):
+        cc, yy = places[i]
+        return lo * 8 + yy * 2 + cc
+
+    def give(i, part=None):
+        cc, yy = places[i]
+        at = lanes(part)
+        pbuf[i, :, at] = jnp.dot(
+            xbuf[cc, yy], wbuf[1 - zl, :, at], preferred_element_type=F32
+        ).astype(BF16)
+        dst = qkv.at[block(zl, i), :, at]
+        send(pbuf.at[i, :, at], dst, to_mate, "mate", i, part)
+
+    lane = lax.broadcasted_iota(jnp.int32, (ROWS, 128), 1)
+    kpos = lax.broadcasted_iota(jnp.int32, (ROWS, 128), 0)
+    mark = lax.broadcasted_iota(jnp.int32, (128 - HD, ROWS), 0)
+    qpos = lax.broadcasted_iota(jnp.int32, (128 - HD, ROWS), 1)
+    cuts = []
+
+    def image_of(pos):
+        return sum((pos >= cut).astype(jnp.int32) for cut in cuts)
+
+    def lay_out(b, heads):
+        rows = pl.ds(pl.multiple_of(b * ROWS, ROWS), ROWS)
+        other = image_of(kpos + b * ROWS) != lane - HD
+        kaug[rows, :] = jnp.where(
+            lane < HD, heads[:, 128:256], jnp.where(other, 1.0, 0.0).astype(BF16)
+        )
+        turned = heads.T
+        own = image_of(qpos + b * ROWS) == mark
+        qaug[0:HD, rows] = turned[0:HD]
+        qaug[HD:128, rows] = jnp.where(own, -1e30, 0.0).astype(BF16)
+        vt[0:48, rows] = turned[80:128]
+        vt[48:80, rows] = turned[208:240]
+
+    def take(i):
+        cc, yy = places[i]
+        heads = jnp.dot(
+            xbuf[cc, yy], wbuf[zl], preferred_element_type=F32
+        ).astype(BF16)
+        lay_out(block(zl, i), heads)
+
+    def receive(i, parts=(None,)):
+        b = block(1 - zl, i)
+        for part in parts:
+            arrived(qkv.at[b, :, lanes(part)], "mate", i, part)
+        lay_out(b, qkv[b])
+
+    loads[2].wait()
+    w_here(theirs, 0)
+    give(0, 0)
+    arrived(xbuf.at[co, y], "c", 0)
+    give(1, 0)
 
     for d in range(1, 8):
         arrived(zbuf.at[behind(d)], "oz", d)
     own_o.wait()
     for zz in range(8):
-        lane = (zz % 2) * 4 * HD + (zz // 2) * HD
-        pack[:, lane : lane + HD] = zbuf[zz][:, :HD]
+        lane0 = (zz % 2) * 4 * HD + (zz // 2) * HD
+        pack[:, lane0 : lane0 + HD] = zbuf[zz][:, :HD]
     for to, k in zip(to_y, range(3)):
         send(pack, wo_ref.at[c, x, y], to, "oy", k)
     own_pack = keep(pack, wo_ref.at[c, x, y])
@@ -129,37 +227,21 @@
     arrived(xpart(c, yp, 1), "y-", 1)
     send(xpart(c, yp, 1), xpart(c, yp, 1), to_y[1], "y2", 1)
 
-    def w_here(ds):
-        for d in ds:
-            for k, xx in enumerate((xm, xp, x2)):
-                arrived(wslot(behind(d), xx), "wx", d, k)
-
-    def block(lo, cc, yy):
-        row = pl.multiple_of((lo * 8 + yy * 2 + cc) * ROWS, ROWS)
-        return qkv_ref.at[pl.ds(row, ROWS), :]
-
-    places = ((c, y), (co, y), (c, ym), (c, yp), (co, ym), (co, yp), (c, y2), (co, y2))
-
-    def project(i, whose):
-        head = zl if whose else 1 - zl
-        cc, yy = places[i]
-        pbuf[i, whose] = jnp.dot(
-            xbuf[cc, yy], wbuf[head], preferred_element_type=F32
-        ).astype(BF16)
-        if whose:
-            keep(pbuf.at[i, 1], block(zl, cc, yy))
-        else:
-            send(pbuf.at[i, 0], block(zl, cc, yy), to_mate, "mate", i)
-
-    w_here((1, 7, 3, 5))
-    own_x.wait()
-    project(0, 0)
-    arrived(xbuf.at[co, y], "c", 0)
-    project(1, 0)
+    w_here(theirs, 1)
+    give(0, 1)
+    give(1, 1)
+    loads[3].wait()
+    for a in (1, 2, 3):
+        count = jnp.sum((ids[...] < a).astype(F32))
+        cuts.append(count.astype(jnp.int32))
+        cut_ref[a - 1 : a, :] = jnp.full((1, 128), count, F32)
+    cut_ref[3:8, :] = jnp.zeros((5, 128), F32)
+    kaug[SEQ : SEQ + CK, :] = jnp.ones((CK, 128), BF16)
+    vt[:, SEQ : SEQ + CK] = jnp.zeros((HD, CK), BF16)
     own_w.wait()
-    w_here((0, 2, 6, 4))
-    project(0, 1)
-    project(1, 1)
+    w_here((0, *ours), None)
+    take(0)
+    take(1)
 
     own_pack.wait()
     for k, yy in enumerate((y, ym, yp, y2)):
@@ -173,14 +255,14 @@
     send(xbuf.at[c, ym], xbuf.at[c, ym], to_co, "c", 1)
     arrived(xpart(c, yp, 0), "y-", 0)
     send(xbuf.at[c, yp], xbuf.at[c, yp], to_co, "c", 2)
-    project(2, 0)
-    project(3, 0)
+    give(2)
+    give(3)
     arrived(xbuf.at[co, ym], "c", 1)
-    project(4, 0)
+    give(4)
     arrived(xbuf.at[co, yp], "c", 2)
-    project(5, 0)
+    give(5)
     for i in (2, 3, 4, 5):
-        project(i, 1)
+        take(i)
 
     for k, yy in enumerate((y, ym, yp, y2)):
         side = k % 2
@@ -191,11 +273,13 @@
     arrived(xpart(c, y2, 0), "y2", 0)
     arrived(xpart(c, y2, 1), "y2", 1)
     send(xbuf.at[c, y2], xbuf.at[c, y2], to_co, "c", 3)
-    project(6, 0)
+    give(6)
     arrived(xbuf.at[co, y2], "c", 3)
-    project(7, 0)
-    project(6, 1)
-    project(7, 1)
+    give(7)
+    take(6)
+    take(7)
+    receive(0, (0, 1))
+    receive(1, (0, 1))
 
     send(wo_ref.at[c, x], wo_ref.at[c, x], to_co, "oc", 0)
     for k, yy in enumerate((y, ym, yp, y2)):
@@ -206,50 +290,47 @@
     for k, yy in enumerate((y, ym, yp, y2)):
         arrived(wo_ref.at[c, x2, yy], "ox", k, 2)
     send(wo_ref.at[c, x2], wo_ref.at[c, x2], to_co, "oc", 3)
-    for i, (cc, yy) in enumerate(places):
-        arrived(block(1 - zl, cc, yy), "mate", i)
+    for i in range(2, 8):
+        receive(i)
     for k, xx in enumerate((x, xm, xp, x2)):
         arrived(wo_ref.at[co, xx], "oc", k)
-    for cp in local[4:]:
-        cp.wait()
     for cp in sent:
         cp.wait_send()
 
 
-def project(patches, w):
+def project(patches, ids, w_qkv, w_out):
     return pl.pallas_call(
         project_kernel,
         out_shape=(
-            jax.ShapeDtypeStruct((SEQ, PACK), BF16),
+            jax.ShapeDtypeStruct((SEQ + CK, 128), BF16),
+            jax.ShapeDtypeStruct((128, SEQ), BF16),
+            jax.ShapeDtypeStruct((HD, SEQ + CK), BF16),
+            jax.ShapeDtypeStruct((8, 128), F32),
             jax.ShapeDtypeStruct((2, 4, 4, HD, 8 * HD), BF16),
         ),
-        in_specs=[
-            pl.BlockSpec(memory_space=pl.ANY),
-            pl.BlockSpec(memory_space=pltpu.VMEM),
-        ],
-        out_specs=(pl.BlockSpec(memory_space=pl.ANY),) * 2,
+        in_specs=[pl.BlockSpec(memory_space=pltpu.HBM)] * 4,
+        out_specs=(pl.BlockSpec(memory_space=pltpu.VMEM),) * 4
+        + (pl.BlockSpec(memory_space=pl.ANY),),
         scratch_shapes=[
+            pltpu.VMEM((SEQ // 128, 128), jnp.int32),
+            pltpu.VMEM((3, HD, HD), BF16),
+            pltpu.VMEM((HD, HD), BF16),
+            pltpu.VMEM((HD, PACK + 128), BF16),
             pltpu.VMEM((2, 4, ROWS, D), BF16),
             pltpu.VMEM((2, D, PACK), BF16),
-            pltpu.VMEM((8, 2, ROWS, PACK), BF16),
+            pltpu.VMEM((8, ROWS, PACK), BF16),
+            pltpu.VMEM((16, ROWS, PACK), BF16),
             pltpu.VMEM((8, HD, 128), BF16),
             pltpu.VMEM((HD, 8 * HD), BF16),
-            pltpu.SemaphoreType.DMA((80,)),
-            pltpu.SemaphoreType.DMA((80,)),
-            pltpu.SemaphoreType.DMA((16,)),
+            pltpu.SemaphoreType.DMA((100,)),
+            pltpu.SemaphoreType.DMA((100,)),
+            pltpu.SemaphoreType.DMA((8,)),
         ],
         compiler_params=pltpu.CompilerParams(
             collective_id=0, has_side_effects=True, vmem_limit_bytes=40 << 20
         ),
         name="project",
-    )(patches, w)
-
-
-TQ = 256
-CK = 768
-SUB = 128
-BLOCKS = SEQ // TQ
-SCALE = math.log2(math.e) / math.sqrt(HD)
+    )(patches, ids, w_qkv, w_out)
 
 
 def rows_fold(op, a):
@@ -261,35 +342,9 @@
 
 
 def attend_kernel(
-    ids_ref, qkv_ref, o_ref, kaug, qaug, vt, s0, s1, e0, e1, acc, state
+    cut_ref, kaug, qaug, vt, o_ref, s0, s1, e0, e1, acc, state
 ):
-    ids = ids_ref[...]
-    cuts = [jnp.sum((ids < a).astype(F32)).astype(jnp.int32) for a in (1, 2, 3)]
-
-    def image_of(pos):
-        return sum((pos >= cut).astype(jnp.int32) for cut in cuts)
-
-    lane = lax.broadcasted_iota(jnp.int32, (TQ, 128), 1)
-    kpos = lax.broadcasted_iota(jnp.int32, (TQ, 128), 0)
-    mark = lax.broadcasted_iota(jnp.int32, (128 - HD, TQ), 0)
-    qpos = lax.broadcasted_iota(jnp.int32, (128 - HD, TQ), 1)
-
-    @pl.loop(0, BLOCKS)
-    def _(i):
-        rows = pl.ds(pl.multiple_of(i * TQ, TQ), TQ)
-        other = image_of(kpos + i * TQ) != lane - HD
-        kaug[rows, :] = jnp.where(
-            lane < HD, qkv_ref[rows, 128:256], jnp.where(other, 1.0, 0.0).astype(BF16)
-        )
-        turned = qkv_ref[rows, :].T
-        own = image_of(qpos + i * TQ) == mark
-        qaug[0:HD, rows] = turned[0:HD]
-        qaug[HD:128, rows] = jnp.where(own, -1e30, 0.0).astype(BF16)
-        vt[0:48, rows] = turned[80:128]
-        vt[48:80, rows] = turned[208:240]
-
-    kaug[SEQ : SEQ + CK, :] = jnp.ones((CK, 128), BF16)
-    vt[:, SEQ : SEQ + CK] = jnp.zeros((HD, CK), BF16)
+    cuts = [jnp.max(cut_ref[a : a + 1, :]).astype(jnp.int32) for a in range(3)]
     for ref in (s0, s1, e0, e1, acc, state):
         ref[...] = jnp.zeros_like(ref)
 
@@ -352,16 +407,13 @@
     lax.fori_loop(0, lax.div(steps + 3, 2), pair, (jnp.int32(0),) * 8)
 
 
-def attend(ids, qkv):
+def attend(cuts, kaug, qaug, vt):
     return pl.pallas_call(
         attend_kernel,
         out_shape=jax.ShapeDtypeStruct((HD, SEQ + TQ), BF16),
-        in_specs=[pl.BlockSpec(memory_space=pltpu.VMEM)] * 2,
+        in_specs=[pl.BlockSpec(memory_space=pltpu.VMEM)] * 4,
         out_specs=pl.BlockSpec(memory_space=pltpu.VMEM),
         scratch_shapes=[
-            pltpu.VMEM((SEQ + CK, 128), BF16),
-            pltpu.VMEM((128, SEQ), BF16),
-            pltpu.VMEM((HD, SEQ + CK), BF16),
             pltpu.VMEM((CK, TQ), F32),
             pltpu.VMEM((CK, TQ), F32),
             pltpu.VMEM((CK, TQ), BF16),
@@ -371,7 +423,7 @@
         ],
         compiler_params=pltpu.CompilerParams(vmem_limit_bytes=40 << 20),
         name="attend",
-    )(ids, qkv)
+    )(cuts, kaug, qaug, vt)
 
 
 def output_kernel(o_ref, wg_ref, out_ref, held, whole, ssem, rsem):
@@ -451,12 +503,9 @@
 
 
 def shards(patches, image_ids, w_qkv, w_out):
-    q, k, v = w_qkv[0], w_qkv[1], w_qkv[2]
-    spare = jnp.zeros((HD, PACK - 3 * HD), BF16)
-    more = jnp.zeros((HD, 128 - HD), BF16)
-    w = jnp.concatenate([q, v[:, :48], k, v[:, 48:], spare, w_out, more], axis=1)
-    qkv, wo = project(patches[0], w)
-    o = attend(image_ids.reshape(SEQ // 128, 128), qkv)
+    ids = image_ids.reshape(SEQ // 128, 128)
+    kaug, qaug, vt, cuts, wo = project(patches[0], ids, w_qkv, w_out)
+    o = attend(cuts, kaug, qaug, vt)
     out = output(o, wo)
     return out[None]
 

time: 81.7 us -> 80.3 us (0.983)
  Pallas kernels: 77 us -> 75.8 us
    pallas_call x1, Pallas kernels: 13.6 us -> 11.7 us  [attend(): pl.pallas_call(attend_kernel, out_shape=jax.ShapeDtypeStruct((HD, SEQ + T...]
    unnamed x5 -> x9, local copies, waits for them, and re-layouts: 2.63 us -> 4.2 us
    pallas_call x1, Pallas kernels: 48.9 us -> 50.1 us  [project(): pl.pallas_call(project_kernel, out_shape=(jax.ShapeDtypeStruct((SEQ + CK,...]
    concatenate x1 -> x0, local copies, waits for them, and re-layouts: 0.84 us -> none  [shards(): jnp.concatenate([q, v[:, :48], k, v[:, 48:], spare, w_out, more], axis=1)]
where the time goes in v4:
time: 80.3 us; the launch traced here: 80 us
  Pallas kernels  75.8 us (94%)
  local copies, waits for them, and re-layouts  4.2 us (5%)
    pallas_call x1, Pallas kernels, project(): pl.pallas_call(project_kernel, out_shape=(jax.ShapeDtypeStruct((SEQ + CK,...  50.1 us
    pallas_call x1, Pallas kernels, output(): pl.pallas_call(output_kernel, out_shape=jax.ShapeDtypeStruct((ROWS, D), B...  14 us
    pallas_call x1, Pallas kernels, attend(): pl.pallas_call(attend_kernel, out_shape=jax.ShapeDtypeStruct((HD, SEQ + T...  11.7 us
    unnamed x9, local copies, waits for them, and re-layouts  4.2 us

profile of v4, /device:TPU:1, one launch (start us, length us, event | category | flops | bytes accessed | tf_op | source)
XLA Modules:
  0.0 80.0 jit_solution(10287579449915788745)
XLA Ops:
  0.0 0.0 copy-start
  0.0 1.1 %copy-done = bf16[1,256,1280]{2,1,0:T(8,128)(2,1)S(1)} copy-done((bf16[1,256,1280]{2,1,0:T(8,128)(2,1)S(1)}, bf16[1,256,1280]{2,1,0:T(8,128)(2,1)}, u32[]{:S(2)}) %copy-start) | copy-done | bytes 655384
  1.1 0.0 copy-start.1
  1.1 0.8 %copy-done.1 = bf16[3,80,80]{2,1,0:T(8,128)(2,1)S(1)} copy-done((bf16[3,80,80]{2,1,0:T(8,128)(2,1)S(1)}, bf16[3,80,80]{2,1,0:T(8,128)(2,1)}, u32[]{:S(2)}) %copy-start.1) | copy-done | bytes 38424
  1.9 0.0 copy-start.2
  1.9 0.7 copy-done.2
  2.6 0.0 copy-start.3
  2.6 0.7 copy-done.3
  3.4 50.1 %project.1 = (bf16[4864,128]{1,0:T(8,128)(2,1)S(1)}, bf16[128,4096]{1,0:T(8,128)(2,1)S(1)}, bf16[80,4864]{1,0:T(8,128)(2,1)S(1)}, f32[8,128]{1,0:T(8,128)S(1)}, bf16[2,4,4,80,640]{4,3,2,1,0:T(8,128)(2,1)S(1)}) custom-call(bf16[256,1280]{1,0:T(8,128)(2,1)S(1)} %bitcast.4, s32[32,128]{1,0:T(8,128)S(1)} %bitcast.5, bf16[3,80,80]{2,1,0:T(8,128)(2,1)S(1)} %copy-done.1, ...), custom_call_target="tpu_custom_call" | custom-call | tf_op jit(solution)/shard_map/project/pallas_call | solution.py:302
  53.5 11.7 %attend.1.o_ref = bf16[80,4352]{1,0:T(8,128)(2,1)S(1)} custom-call(f32[8,128]{1,0:T(8,128)S(1)} %get-tuple-element.10.cut_ref, bf16[4864,128]{1,0:T(8,128)(2,1)S(1)} %get-tuple-element.11.kaug, bf16[128,4096]{1,0:T(8,128)(2,1)S(1)} %get-tuple-element.12.qaug, bf16[80,4864]{1,0:T(8,128)(2,1)S(1)} %get-tuple-element.13.vt), custom_call_target="tpu_custom_call" | custom-call | tf_op jit(solution)/shard_map/attend/pallas_call | solution.py:411
  65.2 14.0 %output.1 = bf16[256,1280]{1,0:T(8,128)(2,1)S(1)} custom-call(bf16[80,4352]{1,0:T(8,128)(2,1)S(1)} %attend.1.o_ref, bf16[2,4,4,80,640]{4,3,2,1,0:T(8,128)(2,1)S(1)} %get-tuple-element.14.wg_ref), custom_call_target="tpu_custom_call" | custom-call | tf_op jit(solution)/shard_map/output/pallas_call | solution.py:487
  79.2 0.8 %copy.6 = bf16[1,256,1280]{2,1,0:T(8,128)(2,1)} copy(bf16[1,256,1280]{2,1,0:T(8,128)(2,1)S(1)} %bitcast.3) | data formatting | bytes 1310720
Async XLA Ops:
  0.0 1.1 %copy-start = (bf16[1,256,1280]{2,1,0:T(8,128)(2,1)S(1)}, bf16[1,256,1280]{2,1,0:T(8,128)(2,1)}, u32[]{:S(2)}) copy-start(bf16[1,256,1280]{2,1,0:T(8,128)(2,1)} %param.4) | copy-start | bytes 1966084
  1.1 0.8 %copy-start.1 = (bf16[3,80,80]{2,1,0:T(8,128)(2,1)S(1)}, bf16[3,80,80]{2,1,0:T(8,128)(2,1)}, u32[]{:S(2)}) copy-start(bf16[3,80,80]{2,1,0:T(8,128)(2,1)} %wqkv_ref.1) | copy-start | bytes 115204
  1.9 0.7 copy-start.2
  2.6 0.7 copy-start.3

commit v5 on v4

--- a/solution.py
+++ b/solution.py
@@ -126,8 +126,7 @@
     for part in (0, 1):
         src = x_ref.at[pl.ds(part * half, half), :]
         send(src, xpart(c, y, part), to_y[0], "y+", part)
-        src = x_ref.at[pl.ds((1 - part) * half, half), :]
-        send(src, xpart(c, y, 1 - part), to_y[1], "y-", 1 - part)
+        send(src, xpart(c, y, part), to_y[1], "y-", part)
     send(x_ref, xbuf.at[c, y], to_co, "c", 0)
     for d in ours:
         send(w_mine(), wslot(z, x), to_z[d], "wz", d, None)
@@ -162,14 +161,19 @@
         cc, yy = places[i]
         return lo * 8 + yy * 2 + cc
 
-    def give(i, part=None):
+    def turned_rows(part):
+        return slice(*((0, 3 * HD), (0, 128), (128, 3 * HD))[0 if part is None else part + 1])
+
+    def give(i, part=None, side=None):
         cc, yy = places[i]
-        at = lanes(part)
-        pbuf[i, :, at] = jnp.dot(
-            xbuf[cc, yy], wbuf[1 - zl, :, at], preferred_element_type=F32
+        rows = slice(0, ROWS) if side is None else slice(side * half, (side + 1) * half)
+        heads = jnp.dot(
+            xbuf[cc, yy, rows], wbuf[1 - zl, :, lanes(part)], preferred_element_type=F32
         ).astype(BF16)
-        dst = qkv.at[block(zl, i), :, at]
-        send(pbuf.at[i, :, at], dst, to_mate, "mate", i, part)
+        at = turned_rows(part)
+        pbuf[i, at, rows] = heads.T[: at.stop - at.start]
+        dst = qkv.at[block(zl, i), at, rows]
+        send(pbuf.at[i, at, rows], dst, to_mate, "mate", i, part, side)
 
     lane = lax.broadcasted_iota(jnp.int32, (ROWS, 128), 1)
     kpos = lax.broadcasted_iota(jnp.int32, (ROWS, 128), 0)
@@ -180,13 +184,12 @@
     def image_of(pos):
         return sum((pos >= cut).astype(jnp.int32) for cut in cuts)
 
-    def lay_out(b, heads):
+    def lay_out(b, keys, turned):
         rows = pl.ds(pl.multiple_of(b * ROWS, ROWS), ROWS)
         other = image_of(kpos + b * ROWS) != lane - HD
         kaug[rows, :] = jnp.where(
-            lane < HD, heads[:, 128:256], jnp.where(other, 1.0, 0.0).astype(BF16)
+            lane < HD, keys, jnp.where(other, 1.0, 0.0).astype(BF16)
         )
-        turned = heads.T
         own = image_of(qpos + b * ROWS) == mark
         qaug[0:HD, rows] = turned[0:HD]
         qaug[HD:128, rows] = jnp.where(own, -1e30, 0.0).astype(BF16)
@@ -198,13 +201,31 @@
         heads = jnp.dot(
             xbuf[cc, yy], wbuf[zl], preferred_element_type=F32
         ).astype(BF16)
-        lay_out(block(zl, i), heads)
-
-    def receive(i, parts=(None,)):
+        lay_out(block(zl, i), heads[:, 128:256], heads.T)
+
+    def receive(i):
         b = block(1 - zl, i)
-        for part in parts:
-            arrived(qkv.at[b, :, lanes(part)], "mate", i, part)
-        lay_out(b, qkv[b])
+        if i < 2:
+            for part in (0, 1):
+                arrived(qkv.at[b, turned_rows(part)], "mate", i, part, None)
+        elif i < 6:
+            arrived(qkv.at[b, turned_rows(None)], "mate", i, None, None)
+        else:
+            for side in (0, 1):
+                rows = slice(side * half, (side + 1) * half)
+                arrived(qkv.at[b, turned_rows(None), rows], "mate", i, None, side)
+        turned = qkv[b]
+        lay_out(b, turned[128:256].T, turned)
+
+    def quarter(yy, k):
+        return xbuf.at[c, yy, pl.ds(k * (half // 2), half // 2), :]
+
+    def pass_on(side):
+        arrived(xpart(c, ym, side), "y+", side)
+        send(quarter(ym, 2 * side), quarter(ym, 2 * side), to_y[0], "y2", 2 * side)
+        arrived(xpart(c, yp, side), "y-", side)
+        k = 2 * side + 1
+        send(quarter(yp, k), quarter(yp, k), to_y[1], "y2", k)
 
     loads[2].wait()
     w_here(theirs, 0)
@@ -222,14 +243,20 @@
         send(pack, wo_ref.at[c, x, y], to, "oy", k)
     own_pack = keep(pack, wo_ref.at[c, x, y])
 
-    arrived(xpart(c, ym, 0), "y+", 0)
-    send(xpart(c, ym, 0), xpart(c, ym, 0), to_y[0], "y2", 0)
-    arrived(xpart(c, yp, 1), "y-", 1)
-    send(xpart(c, yp, 1), xpart(c, yp, 1), to_y[1], "y2", 1)
-
+    pass_on(0)
     w_here(theirs, 1)
     give(0, 1)
     give(1, 1)
+    pass_on(1)
+    send(xbuf.at[c, ym], xbuf.at[c, ym], to_co, "c", 1)
+    send(xbuf.at[c, yp], xbuf.at[c, yp], to_co, "c", 2)
+    give(2)
+    give(3)
+    arrived(xbuf.at[co, ym], "c", 1)
+    give(4)
+    arrived(xbuf.at[co, yp], "c", 2)
+    give(5)
+
     loads[3].wait()
     for a in (1, 2, 3):
         count = jnp.sum((ids[...] < a).astype(F32))
@@ -250,52 +277,37 @@
             arrived(here, "oy", k - 1)
         send(here, here, to_x[0], "ox", k, 0)
         send(here, here, to_x[1], "ox", k, 1)
-
-    arrived(xpart(c, ym, 1), "y+", 1)
-    send(xbuf.at[c, ym], xbuf.at[c, ym], to_co, "c", 1)
-    arrived(xpart(c, yp, 0), "y-", 0)
-    send(xbuf.at[c, yp], xbuf.at[c, yp], to_co, "c", 2)
-    give(2)
-    give(3)
-    arrived(xbuf.at[co, ym], "c", 1)
-    give(4)
-    arrived(xbuf.at[co, yp], "c", 2)
-    give(5)
+    send(wo_ref.at[c, x], wo_ref.at[c, x], to_co, "oc", 0)
     for i in (2, 3, 4, 5):
         take(i)
 
-    for k, yy in enumerate((y, ym, yp, y2)):
-        side = k % 2
-        here = wo_ref.at[c, (xm, xp)[side], yy]
-        arrived(here, "ox", k, side)
-        send(here, here, to_x[side], "ox", k, 2)
-
-    arrived(xpart(c, y2, 0), "y2", 0)
-    arrived(xpart(c, y2, 1), "y2", 1)
-    send(xbuf.at[c, y2], xbuf.at[c, y2], to_co, "c", 3)
-    give(6)
-    arrived(xbuf.at[co, y2], "c", 3)
-    give(7)
+    for side in (0, 1):
+        arrived(quarter(y2, 2 * side), "y2", 2 * side)
+        arrived(quarter(y2, 2 * side + 1), "y2", 2 * side + 1)
+        send(xpart(c, y2, side), xpart(c, y2, side), to_co, "c", 3 + side)
+        give(6, None, side)
+        arrived(xpart(co, y2, side), "c", 3 + side)
+        give(7, None, side)
     take(6)
     take(7)
-    receive(0, (0, 1))
-    receive(1, (0, 1))
-
-    send(wo_ref.at[c, x], wo_ref.at[c, x], to_co, "oc", 0)
+    for i in range(5):
+        receive(i)
+
     for k, yy in enumerate((y, ym, yp, y2)):
-        side = 1 - k % 2
-        arrived(wo_ref.at[c, (xm, xp)[side], yy], "ox", k, side)
+        arrived(wo_ref.at[c, xm, yy], "ox", k, 0)
+        arrived(wo_ref.at[c, xp, yy], "ox", k, 1)
     send(wo_ref.at[c, xm], wo_ref.at[c, xm], to_co, "oc", 1)
     send(wo_ref.at[c, xp], wo_ref.at[c, xp], to_co, "oc", 2)
-    for k, yy in enumerate((y, ym, yp, y2)):
-        arrived(wo_ref.at[c, x2, yy], "ox", k, 2)
-    send(wo_ref.at[c, x2], wo_ref.at[c, x2], to_co, "oc", 3)
-    for i in range(2, 8):
+    for i in (5, 6, 7):
         receive(i)
-    for k, xx in enumerate((x, xm, xp, x2)):
+    for k, xx in enumerate((x, xm, xp)):
         arrived(wo_ref.at[co, xx], "oc", k)
     for cp in sent:
         cp.wait_send()
+
+
+def in_hbm(a):
+    return pltpu.with_memory_space_constraint(a, pltpu.HBM)
 
 
 def project(patches, ids, w_qkv, w_out):
@@ -330,7 +342,7 @@
             collective_id=0, has_side_effects=True, vmem_limit_bytes=40 << 20
         ),
         name="project",
-    )(patches, ids, w_qkv, w_out)
+    )(*(in_hbm(a) for a in (patches, ids, w_qkv, w_out)))
 
 
 def rows_fold(op, a):
@@ -426,59 +438,97 @@
     )(cuts, kaug, qaug, vt)
 
 
-def output_kernel(o_ref, wg_ref, out_ref, held, whole, ssem, rsem):
+def output_kernel(
+    o_ref, wg_ref, out_ref, held, whole, far, total, ssem, rsem, fsend, frecv
+):
+    x, y, z, c = place()
     dp, me = lax.axis_index("dp"), lax.axis_index("seq")
+    zl, co = lax.rem(z, 2), 1 - c
+    sides = lax.rem(x + 3, 4), lax.rem(x + 1, 4)
+    to_x = device(sides[1], y, z, c), device(sides[0], y, z, c)
+    to_co = device(x, y, z, co)
+    offsets = [(dz, k) for dz in (0, 1) for k in range(8)][1:]
+
+    def peer(dz, k, back=False):
+        plane = lax.rem(zl + dz, 2) * 8
+        return plane + lax.rem(lax.rem(me, 8) + (8 - k if back else k), 8)
+
     barrier = pltpu.get_barrier_semaphore()
-    for k in range(1, 16):
-        to = (dp, lax.rem(me + k, 16))
+    for to in (*((dp, peer(*o)) for o in offsets), *to_x):
         pl.semaphore_signal(barrier, inc=1, device_id=to, device_id_type=MESH)
-    pl.semaphore_wait(barrier, 15)
-
-    def mine(k):
-        cols = pl.ds(pl.multiple_of(lax.rem(me + k, 16) * ROWS, ROWS), ROWS)
-        return o_ref.at[:, cols]
+    pl.semaphore_wait(barrier, 17)
+
+    def cols(s):
+        return o_ref.at[:, pl.ds(pl.multiple_of(s * ROWS, ROWS), ROWS)]
 
     def slot(s):
         return held.at[pl.ds(pl.multiple_of(s * HD, 16), HD), :]
 
-    copies = []
-    for k in range(1, 16):
-        cp = pltpu.make_async_remote_copy(
-            src_ref=mine(k),
-            dst_ref=slot(me),
-            send_sem=ssem.at[k],
-            recv_sem=rsem.at[k],
-            device_id=(dp, lax.rem(me + k, 16)),
+    def copy(src, dst, sems, to):
+        return pltpu.make_async_remote_copy(
+            src_ref=src,
+            dst_ref=dst,
+            send_sem=sems[0],
+            recv_sem=sems[1],
+            device_id=to,
             device_id_type=MESH,
         )
-        cp.start()
-        copies.append(cp)
-    own = pltpu.make_async_copy(mine(0), slot(me), ssem.at[0])
+
+    copies = []
+    for n, o in enumerate(offsets):
+        to = peer(*o)
+        copies.append(copy(cols(to), slot(me), (ssem.at[n], rsem.at[n]), (dp, to)))
+        copies[-1].start()
+    for yy in range(4):
+        side = yy % 2
+        copies.append(
+            copy(
+                wg_ref.at[c, sides[side], yy],
+                far.at[c, yy],
+                (fsend.at[yy], frecv.at[yy]),
+                to_x[side],
+            )
+        )
+        copies[-1].start()
+    own = pltpu.make_async_copy(cols(me), slot(me), ssem.at[15])
     own.start()
 
-    @pl.loop(0, 8)
-    def _(i):
-        for zl, x, zh in itertools.product(range(2), range(4), range(4)):
-            row = pl.multiple_of((zl * 8 + i) * HD, 16)
-            col, lane = (zh * 4 + x) * HD, (zl * 4 + zh) * HD
-            whole[pl.ds(row, HD), col : col + HD] = wg_ref[
-                lax.rem(i, 2), x, lax.div(i, 2), :, lane : lane + HD
-            ]
+    def unpack(xx, src):
+        @pl.loop(0, 8)
+        def _(i):
+            block = src[lax.rem(i, 2), lax.div(i, 2)]
+            for plane, zh in itertools.product(range(2), range(4)):
+                row = pl.multiple_of((plane * 8 + i) * HD, 16)
+                col, lane = (zh * 4 + xx) * HD, (plane * 4 + zh) * HD
+                whole[pl.ds(row, HD), col : col + HD] = block[:, lane : lane + HD]
+
+    x2 = lax.rem(x + 2, 4)
+    for xx in range(4):
+        pl.when(xx != x2)(functools.partial(unpack, xx, wg_ref.at[:, xx]))
+    for yy in range(4):
+        copy(far.at[c, yy], far.at[c, yy], (fsend.at[yy], frecv.at[yy]), to_co).wait_recv()
+    copies.append(copy(far.at[c], far.at[c], (fsend.at[4], frecv.at[4]), to_co))
+    copies[-1].start()
+    copy(far.at[co], far.at[co], (fsend.at[4], frecv.at[4]), to_co).wait_recv()
+    for xx in range(4):
+        pl.when(xx == x2)(functools.partial(unpack, xx, far))
+
+    def heads(plane):
+        rows = pl.ds(pl.multiple_of(plane * 8 * HD, 128), 8 * HD)
+        return lax.dot_general(
+            held[rows, :],
+            whole[rows, :],
+            (((0,), (0,)), ((), ())),
+            preferred_element_type=F32,
+        )
 
     own.wait()
-    for k in range(1, 16):
-        frm = slot(lax.rem(me + 16 - k, 16))
-        pltpu.make_async_remote_copy(
-            src_ref=frm,
-            dst_ref=frm,
-            send_sem=ssem.at[k],
-            recv_sem=rsem.at[k],
-            device_id=(dp, lax.rem(me + k, 16)),
-            device_id_type=MESH,
-        ).wait_recv()
-    out_ref[...] = lax.dot_general(
-        held[...], whole[...], (((0,), (0,)), ((), ())), preferred_element_type=F32
-    ).astype(BF16)
+    for n, o in enumerate(offsets):
+        if o[0] == 1 and o[1] == 0:
+            total[...] = heads(zl)
+        frm = slot(peer(*o, back=True))
+        copy(frm, frm, (ssem.at[n], rsem.at[n]), to_co).wait_recv()
+    out_ref[...] = (total[...] + heads(1 - zl)).astype(BF16)
     for cp in copies:
         cp.wait_send()
 
@@ -492,8 +542,12 @@
         scratch_shapes=[
             pltpu.VMEM((D, ROWS), BF16),
             pltpu.VMEM((D, D), BF16),
+            pltpu.VMEM((2, 4, HD, 8 * HD), BF16),
+            pltpu.VMEM((ROWS, D), F32),
             pltpu.SemaphoreType.DMA((16,)),
             pltpu.SemaphoreType.DMA((16,)),
+            pltpu.SemaphoreType.DMA((5,)),
+            pltpu.SemaphoreType.DMA((5,)),
         ],
         compiler_params=pltpu.CompilerParams(
             collective_id=1, has_side_effects=True, vmem_limit_bytes=40 << 20

time: 80.3 us -> 75.9 us (0.945)
  local copies, waits for them, and re-layouts: 4.2 us -> 0.84 us
  Pallas kernels: 75.8 us -> 74.9 us
    unnamed x9 -> x1, local copies, waits for them, and re-layouts: 4.2 us -> 0.84 us
    pallas_call x1, Pallas kernels: 50.1 us -> 46.8 us  [project(): pl.pallas_call(project_kernel, out_shape=(jax.ShapeDtypeStruct((SEQ + CK,...]
    pallas_call x1, Pallas kernels: 14 us -> 16.3 us  [output(): pl.pallas_call(output_kernel, out_shape=jax.ShapeDtypeStruct((ROWS, D), B...]
where the time goes in v5:
time: 75.9 us; the launch traced here: 75.8 us
  Pallas kernels  74.9 us (99%)
  local copies, waits for them, and re-layouts  0.84 us (1%)
    pallas_call x1, Pallas kernels, project(): pl.pallas_call(project_kernel, out_shape=(jax.ShapeDtypeStruct((SEQ + CK,...  46.8 us
    pallas_call x1, Pallas kernels, output(): pl.pallas_call(output_kernel, out_shape=jax.ShapeDtypeStruct((ROWS, D), B...  16.3 us
    pallas_call x1, Pallas kernels, attend(): pl.pallas_call(attend_kernel, out_shape=jax.ShapeDtypeStruct((HD, SEQ + T...  11.9 us

profile of v5, /device:TPU:1, one launch (start us, length us, event | category | flops | bytes accessed | tf_op | source)
XLA Modules:
  0.0 75.8 jit_solution(12676609776081550863)
XLA Ops:
  0.0 46.8 %project.1 = (bf16[4864,128]{1,0:T(8,128)(2,1)S(1)}, bf16[128,4096]{1,0:T(8,128)(2,1)S(1)}, bf16[80,4864]{1,0:T(8,128)(2,1)S(1)}, f32[8,128]{1,0:T(8,128)S(1)}, bf16[2,4,4,80,640]{4,3,2,1,0:T(8,128)(2,1)S(1)}) custom-call(bf16[256,1280]{1,0:T(8,128)(2,1)} %bitcast.4, s32[32,128]{1,0:T(8,128)} %bitcast.5, bf16[3,80,80]{2,1,0:T(8,128)(2,1)} %wqkv_ref.1, ...), custom_call_target="tpu_custom_call" | custom-call | tf_op jit(solution)/shard_map/project/pallas_call | solution.py:314
  46.8 11.9 %attend.1.o_ref = bf16[80,4352]{1,0:T(8,128)(2,1)S(1)} custom-call(f32[8,128]{1,0:T(8,128)S(1)} %get-tuple-element.10.cut_ref, bf16[4864,128]{1,0:T(8,128)(2,1)S(1)} %get-tuple-element.11.kaug, bf16[128,4096]{1,0:T(8,128)(2,1)S(1)} %get-tuple-element.12.qaug, bf16[80,4864]{1,0:T(8,128)(2,1)S(1)} %get-tuple-element.13.vt), custom_call_target="tpu_custom_call" | custom-call | tf_op jit(solution)/shard_map/attend/pallas_call | solution.py:423
  58.7 16.3 %output.1 = bf16[256,1280]{1,0:T(8,128)(2,1)S(1)} custom-call(bf16[80,4352]{1,0:T(8,128)(2,1)S(1)} %attend.1.o_ref, bf16[2,4,4,80,640]{4,3,2,1,0:T(8,128)(2,1)S(1)} %get-tuple-element.14.wg_ref), custom_call_target="tpu_custom_call" | custom-call | tf_op jit(solution)/shard_map/output/pallas_call | solution.py:537
  75.0 0.8 %copy.6 = bf16[1,256,1280]{2,1,0:T(8,128)(2,1)} copy(bf16[1,256,1280]{2,1,0:T(8,128)(2,1)S(1)} %bitcast.3) | data formatting | bytes 1310720

commit v6 on v5

--- a/solution.py
+++ b/solution.py
@@ -296,12 +296,9 @@
     for k, yy in enumerate((y, ym, yp, y2)):
         arrived(wo_ref.at[c, xm, yy], "ox", k, 0)
         arrived(wo_ref.at[c, xp, yy], "ox", k, 1)
-    send(wo_ref.at[c, xm], wo_ref.at[c, xm], to_co, "oc", 1)
-    send(wo_ref.at[c, xp], wo_ref.at[c, xp], to_co, "oc", 2)
     for i in (5, 6, 7):
         receive(i)
-    for k, xx in enumerate((x, xm, xp)):
-        arrived(wo_ref.at[co, xx], "oc", k)
+    arrived(wo_ref.at[co, x], "oc", 0)
     for cp in sent:
         cp.wait_send()
 
@@ -439,7 +436,7 @@
 
 
 def output_kernel(
-    o_ref, wg_ref, out_ref, held, whole, far, total, ssem, rsem, fsend, frecv
+    o_ref, wg_ref, out_ref, held, whole, far, near, total, ssem, rsem, fsend, frecv
 ):
     x, y, z, c = place()
     dp, me = lax.axis_index("dp"), lax.axis_index("seq")
@@ -447,7 +444,7 @@
     sides = lax.rem(x + 3, 4), lax.rem(x + 1, 4)
     to_x = device(sides[1], y, z, c), device(sides[0], y, z, c)
     to_co = device(x, y, z, co)
-    offsets = [(dz, k) for dz in (0, 1) for k in range(8)][1:]
+    offsets = [(dz, k) for dz in (1, 0) for k in range(8) if dz or k]
 
     def peer(dz, k, back=False):
         plane = lax.rem(zl + dz, 2) * 8
@@ -475,10 +472,6 @@
         )
 
     copies = []
-    for n, o in enumerate(offsets):
-        to = peer(*o)
-        copies.append(copy(cols(to), slot(me), (ssem.at[n], rsem.at[n]), (dp, to)))
-        copies[-1].start()
     for yy in range(4):
         side = yy % 2
         copies.append(
@@ -490,28 +483,43 @@
             )
         )
         copies[-1].start()
+    for n, o in enumerate(offsets):
+        to = peer(*o)
+        copies.append(copy(cols(to), slot(me), (ssem.at[n], rsem.at[n]), (dp, to)))
+        copies[-1].start()
+    crossing = []
+    for side in (0, 1):
+        sems = fsend.at[5 + side], frecv.at[5 + side]
+        copies.append(copy(wg_ref.at[c, sides[side]], near.at[side], sems, to_co))
+        copies[-1].start()
+        crossing.append(copy(near.at[side], near.at[side], sems, to_co))
     own = pltpu.make_async_copy(cols(me), slot(me), ssem.at[15])
     own.start()
 
-    def unpack(xx, src):
-        @pl.loop(0, 8)
-        def _(i):
-            block = src[lax.rem(i, 2), lax.div(i, 2)]
-            for plane, zh in itertools.product(range(2), range(4)):
-                row = pl.multiple_of((plane * 8 + i) * HD, 16)
-                col, lane = (zh * 4 + xx) * HD, (plane * 4 + zh) * HD
-                whole[pl.ds(row, HD), col : col + HD] = block[:, lane : lane + HD]
-
-    x2 = lax.rem(x + 2, 4)
-    for xx in range(4):
-        pl.when(xx != x2)(functools.partial(unpack, xx, wg_ref.at[:, xx]))
+    def unpack(xx, ours, others):
+        @pl.loop(0, 4)
+        def _(yy):
+            for core, src in ((c, ours), (co, others)):
+                block = src[yy]
+                for plane, zh in itertools.product(range(2), range(4)):
+                    row = pl.multiple_of((plane * 8 + yy * 2 + core) * HD, 16)
+                    col, lane = (zh * 4 + xx) * HD, (plane * 4 + zh) * HD
+                    whole[pl.ds(row, HD), col : col + HD] = block[:, lane : lane + HD]
+
+    def unpack_if(where, ours, others):
+        for xx in range(4):
+            pl.when(xx == where)(functools.partial(unpack, xx, ours, others))
+
+    unpack_if(x, wg_ref.at[c, x], wg_ref.at[co, x])
+    for side in (0, 1):
+        crossing[side].wait_recv()
+        unpack_if(sides[side], wg_ref.at[c, sides[side]], near.at[side])
     for yy in range(4):
         copy(far.at[c, yy], far.at[c, yy], (fsend.at[yy], frecv.at[yy]), to_co).wait_recv()
     copies.append(copy(far.at[c], far.at[c], (fsend.at[4], frecv.at[4]), to_co))
     copies[-1].start()
     copy(far.at[co], far.at[co], (fsend.at[4], frecv.at[4]), to_co).wait_recv()
-    for xx in range(4):
-        pl.when(xx == x2)(functools.partial(unpack, xx, far))
+    unpack_if(lax.rem(x + 2, 4), far.at[c], far.at[co])
 
     def heads(plane):
         rows = pl.ds(pl.multiple_of(plane * 8 * HD, 128), 8 * HD)
@@ -524,11 +532,11 @@
 
     own.wait()
     for n, o in enumerate(offsets):
-        if o[0] == 1 and o[1] == 0:
-            total[...] = heads(zl)
+        if o == (0, 1):
+            total[...] = heads(1 - zl)
         frm = slot(peer(*o, back=True))
         copy(frm, frm, (ssem.at[n], rsem.at[n]), to_co).wait_recv()
-    out_ref[...] = (total[...] + heads(1 - zl)).astype(BF16)
+    out_ref[...] = (total[...] + heads(zl)).astype(BF16)
     for cp in copies:
         cp.wait_send()
 
@@ -543,11 +551,12 @@
             pltpu.VMEM((D, ROWS), BF16),
             pltpu.VMEM((D, D), BF16),
             pltpu.VMEM((2, 4, HD, 8 * HD), BF16),
+            pltpu.VMEM((2, 4, HD, 8 * HD), BF16),
             pltpu.VMEM((ROWS, D), F32),
             pltpu.SemaphoreType.DMA((16,)),
             pltpu.SemaphoreType.DMA((16,)),
-            pltpu.SemaphoreType.DMA((5,)),
-            pltpu.SemaphoreType.DMA((5,)),
+            pltpu.SemaphoreType.DMA((7,)),
+            pltpu.SemaphoreType.DMA((7,)),
         ],
         compiler_params=pltpu.CompilerParams(
             collective_id=1, has_side_effects=True, vmem_limit_bytes=40 << 20

time: 75.9 us -> 73.9 us (0.974)
  Pallas kernels: 74.9 us -> 73.5 us
    pallas_call x1, Pallas kernels: 46.8 us -> 45.3 us  [project(): pl.pallas_call(project_kernel, out_shape=(jax.ShapeDtypeStruct((SEQ + CK,...]
where the time goes in v6:
time: 73.9 us; the launch traced here: 74.4 us
  Pallas kernels  73.5 us (99%)
  local copies, waits for them, and re-layouts  0.84 us (1%)
    pallas_call x1, Pallas kernels, project(): pl.pallas_call(project_kernel, out_shape=(jax.ShapeDtypeStruct((SEQ + CK,...  45.3 us
    pallas_call x1, Pallas kernels, output(): pl.pallas_call(output_kernel, out_shape=jax.ShapeDtypeStruct((ROWS, D), B...  16.9 us
    pallas_call x1, Pallas kernels, attend(): pl.pallas_call(attend_kernel, out_shape=jax.ShapeDtypeStruct((HD, SEQ + T...  11.4 us

profile of v6, /device:TPU:1, one launch (start us, length us, event | category | flops | bytes accessed | tf_op | source)
XLA Modules:
  0.0 74.4 jit_solution(8878831248904477376)
XLA Ops:
  0.0 45.3 %project.1 = (bf16[4864,128]{1,0:T(8,128)(2,1)S(1)}, bf16[128,4096]{1,0:T(8,128)(2,1)S(1)}, bf16[80,4864]{1,0:T(8,128)(2,1)S(1)}, f32[8,128]{1,0:T(8,128)S(1)}, bf16[2,4,4,80,640]{4,3,2,1,0:T(8,128)(2,1)S(1)}) custom-call(bf16[256,1280]{1,0:T(8,128)(2,1)} %bitcast.4, s32[32,128]{1,0:T(8,128)} %bitcast.5, bf16[3,80,80]{2,1,0:T(8,128)(2,1)} %wqkv_ref.1, ...), custom_call_target="tpu_custom_call" | custom-call | tf_op jit(solution)/shard_map/project/pallas_call | solution.py:311
  45.3 11.4 %attend.1.o_ref = bf16[80,4352]{1,0:T(8,128)(2,1)S(1)} custom-call(f32[8,128]{1,0:T(8,128)S(1)} %get-tuple-element.10.cut_ref, bf16[4864,128]{1,0:T(8,128)(2,1)S(1)} %get-tuple-element.11.kaug, bf16[128,4096]{1,0:T(8,128)(2,1)S(1)} %get-tuple-element.12.qaug, bf16[80,4864]{1,0:T(8,128)(2,1)S(1)} %get-tuple-element.13.vt), custom_call_target="tpu_custom_call" | custom-call | tf_op jit(solution)/shard_map/attend/pallas_call | solution.py:420
  56.7 16.9 %output.1 = bf16[256,1280]{1,0:T(8,128)(2,1)S(1)} custom-call(bf16[80,4352]{1,0:T(8,128)(2,1)S(1)} %attend.1.o_ref, bf16[2,4,4,80,640]{4,3,2,1,0:T(8,128)(2,1)S(1)} %get-tuple-element.14.wg_ref), custom_call_target="tpu_custom_call" | custom-call | tf_op jit(solution)/shard_map/output/pallas_call | solution.py:545
  73.5 0.8 %copy.6 = bf16[1,256,1280]{2,1,0:T(8,128)(2,1)} copy(bf16[1,256,1280]{2,1,0:T(8,128)(2,1)S(1)} %bitcast.3) | data formatting | bytes 1310720

commit v7 on v6

--- a/solution.py
+++ b/solution.py
@@ -241,6 +241,8 @@
         pack[:, lane0 : lane0 + HD] = zbuf[zz][:, :HD]
     for to, k in zip(to_y, range(3)):
         send(pack, wo_ref.at[c, x, y], to, "oy", k)
+    send(pack, wo_ref.at[c, x, y], to_x[0], "ox", 0, 0)
+    send(pack, wo_ref.at[c, x, y], to_x[1], "ox", 0, 1)
     own_pack = keep(pack, wo_ref.at[c, x, y])
 
     pass_on(0)
@@ -273,8 +275,9 @@
     own_pack.wait()
     for k, yy in enumerate((y, ym, yp, y2)):
         here = wo_ref.at[c, x, yy]
-        if k:
-            arrived(here, "oy", k - 1)
+        if not k:
+            continue
+        arrived(here, "oy", k - 1)
         send(here, here, to_x[0], "ox", k, 0)
         send(here, here, to_x[1], "ox", k, 1)
     send(wo_ref.at[c, x], wo_ref.at[c, x], to_co, "oc", 0)

time: 73.9 us -> 73.9 us (level)
    pallas_call x1, Pallas kernels: 16.9 us -> 15.8 us  [output(): pl.pallas_call(output_kernel, out_shape=jax.ShapeDtypeStruct((ROWS, D), B...]
    pallas_call x1, Pallas kernels: 11.4 us -> 12.5 us  [attend(): pl.pallas_call(attend_kernel, out_shape=jax.ShapeDtypeStruct((HD, SEQ + T...]
where the time goes in v7:
time: 73.9 us; the launch traced here: 74.4 us
  Pallas kernels  73.5 us (99%)
  local copies, waits for them, and re-layouts  0.84 us (1%)
    pallas_call x1, Pallas kernels, project(): pl.pallas_call(project_kernel, out_shape=(jax.ShapeDtypeStruct((SEQ + CK,...  45.3 us
    pallas_call x1, Pallas kernels, output(): pl.pallas_call(output_kernel, out_shape=jax.ShapeDtypeStruct((ROWS, D), B...  15.8 us
    pallas_call x1, Pallas kernels, attend(): pl.pallas_call(attend_kernel, out_shape=jax.ShapeDtypeStruct((HD, SEQ + T...  12.5 us

profile of v7, /device:TPU:1, one launch (start us, length us, event | category | flops | bytes accessed | tf_op | source)
XLA Modules:
  0.0 74.4 jit_solution(7187049237346118797)
XLA Ops:
  0.0 45.3 %project.1 = (bf16[4864,128]{1,0:T(8,128)(2,1)S(1)}, bf16[128,4096]{1,0:T(8,128)(2,1)S(1)}, bf16[80,4864]{1,0:T(8,128)(2,1)S(1)}, f32[8,128]{1,0:T(8,128)S(1)}, bf16[2,4,4,80,640]{4,3,2,1,0:T(8,128)(2,1)S(1)}) custom-call(bf16[256,1280]{1,0:T(8,128)(2,1)} %bitcast.4, s32[32,128]{1,0:T(8,128)} %bitcast.5, bf16[3,80,80]{2,1,0:T(8,128)(2,1)} %wqkv_ref.1, ...), custom_call_target="tpu_custom_call" | custom-call | tf_op jit(solution)/shard_map/project/pallas_call | solution.py:314
  45.3 12.5 %attend.1.o_ref = bf16[80,4352]{1,0:T(8,128)(2,1)S(1)} custom-call(f32[8,128]{1,0:T(8,128)S(1)} %get-tuple-element.10.cut_ref, bf16[4864,128]{1,0:T(8,128)(2,1)S(1)} %get-tuple-element.11.kaug, bf16[128,4096]{1,0:T(8,128)(2,1)S(1)} %get-tuple-element.12.qaug, bf16[80,4864]{1,0:T(8,128)(2,1)S(1)} %get-tuple-element.13.vt), custom_call_target="tpu_custom_call" | custom-call | tf_op jit(solution)/shard_map/attend/pallas_call | solution.py:423
  57.8 15.8 %output.1 = bf16[256,1280]{1,0:T(8,128)(2,1)S(1)} custom-call(bf16[80,4352]{1,0:T(8,128)(2,1)S(1)} %attend.1.o_ref, bf16[2,4,4,80,640]{4,3,2,1,0:T(8,128)(2,1)S(1)} %get-tuple-element.14.wg_ref), custom_call_target="tpu_custom_call" | custom-call | tf_op jit(solution)/shard_map/output/pallas_call | solution.py:548
  73.5 0.8 %copy.6 = bf16[1,256,1280]{2,1,0:T(8,128)(2,1)} copy(bf16[1,256,1280]{2,1,0:T(8,128)(2,1)S(1)} %bitcast.3) | data formatting | bytes 1310720
